TPU v7x, 32 devices: a whole 2x2x4 slice. The times are simulated.
32 devices in a mesh: corr: 4 (over y, x), tile: 8 (over z, core).
Axes of the slice: x: 2, y: 2, z: 4, core: 2. Of those that a mesh axis runs over, the one named last changes fastest.
Arguments:
- visibilities: bfloat16 [2048, 8, 256], P(('corr', 'tile')), may hold values from -6 to 6
- coords: float32 [2048, 3, 256], P(('corr', 'tile')), may hold values from -12 to 12
- stations: int32 [2048, 2], P(('corr', 'tile')), may hold values from 0 to 511
- tile_ids: int32 [2048, 1], P(('corr', 'tile')), may hold values from 0 to 63; in each aligned block of 64 rows (0 to 63, 64 to 127, ...) at most 2 rows name the same one
- offsets: int32 [2048, 2], P(('corr', 'tile')), may hold values from 0 to 96
- screens: bfloat16 [512, 8, 1024], P('tile'), may hold values from -4 to 4
Outputs:
- grid_tiles: float32 [4, 64, 2, 128, 128], P('corr', 'tile')
Inputs may be any that keep to these rules, and one draw needn't show every extreme that they name: `tile_ids`: within the rows of one device (aligned blocks of 64 rows) no uv-tile is named more than 2 times, and some uv-tile exactly 2 times.
All inputs are finite; a program needn't handle non-finite values.
Results may differ from a plain program's by a relative error of at most 0.0061.
Values may be sent and summed in bfloat16 or wider, within the bound.
No kernel may reach another device: no remote copies, remote signals or barrier semaphores. Data moves between devices by JAX's collectives and lax.ppermute only.
A program may use at most 64 MiB of HBM per device.

v0:
```python
import functools
import math

import jax
import jax.numpy as jnp
import numpy as np
from jax import lax
from jax.experimental import pallas as pl
from jax.experimental.pallas import tpu as pltpu
from jax.sharding import PartitionSpec as P

SUB = 32
NT = 64
TILE_SIDE = 128
PIX = SUB * SUB
LANES = 128
VMEM_LIMIT = 48 * 1024 * 1024

ROOT2 = math.sqrt(2.0)


def half_turn_series():
    grid = np.cos(np.pi * (np.arange(400) + 0.5) / 800.0) * 0.5
    z = grid * grid
    sine = np.polynomial.polynomial.Polynomial.fit(z, np.sin(np.pi * grid) / grid, 4, domain=[0, 0.25], window=[0, 0.25]).coef
    cosine = np.polynomial.polynomial.Polynomial.fit(z, np.cos(np.pi * grid), 4, domain=[0, 0.25], window=[0, 0.25]).coef
    return [float(x) * ROOT2 for x in sine], [float(x) * ROOT2 for x in cosine]


SINE, COSINE = half_turn_series()


def horner(coefficients, z):
    total = coefficients[-1]
    for value in coefficients[-2::-1]:
        total = total * z + value
    return total


def cis_turns(turns):
    t = turns - jnp.round(turns)
    z = t * t
    s = t * horner(SINE, z)
    c = horner(COSINE, z)
    return 1.0 - s * s, s * c


def image_kernel(ncorr, groups, vis_ref, coord_ref, out_ref, square):
    step = vis_ref.shape[0]
    nvis = vis_ref.shape[2]
    centred = (lax.broadcasted_iota(jnp.int32, (SUB, nvis), 0) - SUB // 2).astype(jnp.float32) * (1.0 / SUB)
    bend = 0.5 * centred * centred
    rows = ncorr * SUB

    def one(s):
        u = coord_ref[s, 0:1, :]
        v = coord_ref[s, 1:2, :]
        w = coord_ref[s, 2:3, :]
        sag = w * bend
        e_re, e_im = cis_turns(u * centred - sag)
        f_re, f_im = cis_turns(v * centred - sag)
        vis = vis_ref[s].astype(jnp.float32)
        g_re = []
        g_im = []
        for e in range(ncorr):
            vr = vis[e : e + 1]
            vi = vis[ncorr + e : ncorr + e + 1]
            g_re.append((vr * e_re - vi * e_im).astype(jnp.bfloat16))
            g_im.append((vr * e_im + vi * e_re).astype(jnp.bfloat16))
        left = jnp.concatenate([jnp.concatenate(g_re, axis=0), jnp.concatenate(g_im, axis=0)], axis=1)
        f_re = f_re.astype(jnp.bfloat16)
        f_im = f_im.astype(jnp.bfloat16)
        right = jnp.concatenate(
            [jnp.concatenate([f_re, f_im], axis=0), jnp.concatenate([-f_im, f_re], axis=0)], axis=1
        )
        image = lax.dot_general(left, right, (((1,), (1,)), ((), ())), preferred_element_type=jnp.float32)
        square[pl.ds(pl.multiple_of(s * rows, rows), rows), 0 : 2 * SUB] = image

    def several(i, carry):
        for j in range(4):
            one(i * 4 + j)
        return carry

    lax.fori_loop(0, step // 4, several, 0)

    lane = lax.broadcasted_iota(jnp.int32, (step, LANES), 1)
    per_tile = LANES // SUB
    halves = SUB // groups // per_tile
    for g in range(groups):
        for h in range(halves):
            for e in range(ncorr):
                real = None
                imag = None
                for j in range(per_tile):
                    r = (g * halves + h) * per_tile + j
                    piece = square[pl.ds(e * SUB + r, step, stride=rows), :]
                    a = piece if j == 0 else pltpu.roll(piece, SUB * j, 1)
                    b = piece if j == 1 else pltpu.roll(piece, (SUB * (j - 1)) % LANES, 1)
                    keep = lane < SUB * (j + 1)
                    real = a if real is None else jnp.where(lane < SUB * j, real, a)
                    imag = b if imag is None else jnp.where(lane < SUB * j, imag, b)
                base = h * 2 * ncorr * LANES
                out_ref[g, :, base + e * LANES : base + (e + 1) * LANES] = real.astype(jnp.bfloat16)
                out_ref[g, :, base + (ncorr + e) * LANES : base + (ncorr + e + 1) * LANES] = imag.astype(jnp.bfloat16)


def make_images(visibilities, coords, groups):
    count, fields, nvis = visibilities.shape
    ncorr = fields // 2
    step = 16
    width = fields * PIX // groups
    return pl.pallas_call(
        functools.partial(image_kernel, ncorr, groups),
        grid=(count // step,),
        in_specs=[
            pl.BlockSpec((step, fields, nvis), lambda i: (i, 0, 0)),
            pl.BlockSpec((step, 3, nvis), lambda i: (i, 0, 0)),
        ],
        out_specs=pl.BlockSpec((groups, step, width), lambda i: (0, i, 0)),
        out_shape=jax.ShapeDtypeStruct((groups, count, width), jnp.bfloat16),
        scratch_shapes=[pltpu.VMEM((step * ncorr * SUB, LANES), jnp.float32)],
        compiler_params=pltpu.CompilerParams(vmem_limit_bytes=VMEM_LIMIT),
        cost_estimate=pl.CostEstimate(flops=count * 2 * 128 * 512 * 256, bytes_accessed=2 << 20, transcendentals=0),
        name="images",
    )(visibilities, coords)


def owner_targets(tiles, owners, per_owner, capacity):
    n = tiles.shape[1]
    mine = lax.broadcasted_iota(jnp.int32, (owners, n), 0) == tiles // per_owner
    hot = mine.astype(jnp.float32).astype(jnp.bfloat16)
    before = lax.broadcasted_iota(jnp.int32, (n, n), 0) < lax.broadcasted_iota(jnp.int32, (n, n), 1)
    before = before.astype(jnp.float32).astype(jnp.bfloat16)
    ahead = jnp.dot(hot, before, preferred_element_type=jnp.float32)
    first = (lax.broadcasted_iota(jnp.int32, (owners, n), 0) * capacity).astype(jnp.float32)
    return jnp.sum(jnp.where(mine, ahead + first, 0.0), axis=0, keepdims=True)


def aterm_kernel(ncorr, owners, per_owner, capacity, stations_ref, tiles_ref, taper_ref, image_ref, screen_ref, out_ref, near_ref, far_ref, block_ref):
    n = image_ref.shape[0]
    nst = screen_ref.shape[0]
    number = lax.broadcasted_iota(jnp.int32, (n, nst), 1)
    for column, ref in ((0, near_ref), (1, far_ref)):
        pick = (number == stations_ref[:, column : column + 1]).astype(jnp.float32).astype(jnp.bfloat16)
        ref[...] = jnp.dot(pick, screen_ref[...], preferred_element_type=jnp.float32)
    taper = taper_ref[0]
    chunk = 16

    def part(ref, rows, field):
        return ref[rows, field * LANES : (field + 1) * LANES].astype(jnp.float32)

    def body(i, carry):
        rows = pl.ds(pl.multiple_of(i * chunk, chunk), chunk)
        image_re = [part(image_ref, rows, e) for e in range(ncorr)]
        image_im = [part(image_ref, rows, ncorr + e) for e in range(ncorr)]
        for row_out in range(2):
            mid_re = []
            mid_im = []
            for inner in range(2):
                m_re = 0.0
                m_im = 0.0
                for first in range(2):
                    near_re = part(near_ref, rows, 2 * first + row_out)
                    near_im = part(near_ref, rows, ncorr + 2 * first + row_out)
                    vis_re = image_re[2 * first + inner]
                    vis_im = image_im[2 * first + inner]
                    m_re = m_re + near_re * vis_re + near_im * vis_im
                    m_im = m_im + near_re * vis_im - near_im * vis_re
                mid_re.append(m_re)
                mid_im.append(m_im)
            for col_out in range(2):
                t_re = 0.0
                t_im = 0.0
                for inner in range(2):
                    far_re = part(far_ref, rows, 2 * inner + col_out)
                    far_im = part(far_ref, rows, ncorr + 2 * inner + col_out)
                    t_re = t_re + mid_re[inner] * far_re - mid_im[inner] * far_im
                    t_im = t_im + mid_re[inner] * far_im + mid_im[inner] * far_re
                place = 2 * (2 * row_out + col_out) * LANES
                block_ref[rows, place : place + LANES] = (t_re * taper).astype(jnp.bfloat16)
                block_ref[rows, place + LANES : place + 2 * LANES] = (t_im * taper).astype(jnp.bfloat16)
        return carry

    lax.fori_loop(0, n // chunk, body, 0)
    target = owner_targets(tiles_ref[...], owners, per_owner, capacity)
    slots = lax.broadcasted_iota(jnp.int32, (owners * capacity, n), 0).astype(jnp.float32)
    move = (slots == target).astype(jnp.float32).astype(jnp.bfloat16)
    for e in range(ncorr):
        moved = jnp.dot(move, block_ref[:, 2 * e * LANES : 2 * (e + 1) * LANES], preferred_element_type=jnp.float32)
        out_ref[e] = moved.astype(jnp.bfloat16)


def apply_aterms(images, screens, stations, tiles, taper, ncorr, owners, per_owner, capacity):
    n = images.shape[0]
    nst = screens.shape[0]
    fields = 2 * ncorr
    halves = images.shape[1] // (fields * LANES)
    half = fields * LANES
    return pl.pallas_call(
        functools.partial(aterm_kernel, ncorr, owners, per_owner, capacity),
        grid=(halves,),
        in_specs=[
            pl.BlockSpec((n, 2), lambda h: (0, 0)),
            pl.BlockSpec((1, n), lambda h: (0, 0)),
            pl.BlockSpec((1, 1, LANES), lambda h: (h, 0, 0)),
            pl.BlockSpec((n, half), lambda h: (0, h)),
            pl.BlockSpec((nst, half), lambda h: (0, h)),
        ],
        out_specs=pl.BlockSpec((ncorr, owners * capacity, 2 * LANES), lambda h: (0, 0, h)),
        out_shape=jax.ShapeDtypeStruct((ncorr, owners * capacity, halves * 2 * LANES), jnp.bfloat16),
        scratch_shapes=[
            pltpu.VMEM((n, half), jnp.float32),
            pltpu.VMEM((n, half), jnp.float32),
            pltpu.VMEM((n, half), jnp.bfloat16),
        ],
        compiler_params=pltpu.CompilerParams(vmem_limit_bytes=VMEM_LIMIT),
        name="aterms",
    )(stations, tiles, taper, images, screens)


def places_kernel(owners, per_owner, capacity, tiles_ref, offset_ref, out_ref):
    me = lax.axis_index("tile")
    sources = tiles_ref.shape[0]
    n = tiles_ref.shape[2]
    for t in range(sources):
        tiles = tiles_ref[t]
        target = owner_targets(tiles, owners, per_owner, capacity)
        slots = lax.broadcasted_iota(jnp.int32, (capacity, n), 0) + me * capacity
        hit = (slots.astype(jnp.float32) == target).astype(jnp.float32).astype(jnp.bfloat16)
        local = jnp.where(tiles // per_owner == me, tiles - me * per_owner, 0).astype(jnp.float32)
        used = jnp.where(tiles // per_owner == me, 1.0, 0.0)
        total = jnp.broadcast_to(jnp.sum(used, axis=1, keepdims=True), (1, n))
        offsets = offset_ref[t].astype(jnp.float32)
        values = jnp.concatenate([offsets, local, used, jnp.zeros((4, n), jnp.float32)], axis=0).astype(jnp.bfloat16)
        found = lax.dot_general(values, hit, (((1,), (1,)), ((), ())), preferred_element_type=jnp.float32)
        row = lax.broadcasted_iota(jnp.int32, found.shape, 0)
        out_ref[t] = jnp.where(row == 4, total[:, :capacity], found).astype(jnp.int32)


def find_places(tiles, offsets, owners, per_owner, capacity):
    sources = tiles.shape[0]
    return pl.pallas_call(
        functools.partial(places_kernel, owners, per_owner, capacity),
        out_shape=jax.ShapeDtypeStruct((sources, 8, capacity), jnp.int32),
        compiler_params=pltpu.CompilerParams(vmem_limit_bytes=VMEM_LIMIT),
        name="places",
    )(tiles, offsets)


def grid_kernel(sources, capacity, place_ref, block_ref, factor_ref, out_ref, uv_ref):
    step = pl.program_id(0)
    groups = block_ref.shape[0]
    depth = block_ref.shape[2]
    rows = block_ref.shape[1]
    width = factor_ref.shape[1]
    per_slot = 2 * PIX // LANES
    total = None
    for g in range(groups):
        part = jnp.dot(
            block_ref[g], factor_ref[g * depth : (g + 1) * depth, :], preferred_element_type=jnp.float32
        )
        total = part if total is None else total + part
    for j in range(width // LANES):
        uv_ref[pl.ds(step * (width // LANES) + j, rows, stride=per_slot), :] = total[:, j * LANES : (j + 1) * LANES]

    @pl.when(step == pl.num_programs(0) - 1)
    def _():
        out_ref[...] = jnp.zeros_like(out_ref)
        lane = lax.broadcasted_iota(jnp.int32, (8, LANES), 1)
        pieces = LANES // SUB

        for t in range(sources):

            def add(j, carry):
                x = place_ref[t, 0, j]
                y = place_ref[t, 1, j]
                k = place_ref[t, 2, j]
                inside = (lane >= y) & (lane < y + SUB)
                base = pl.multiple_of((t * capacity + j) * per_slot, per_slot)
                new = []
                for part in range(2):
                    block = uv_ref[pl.ds(base + part * 8, 8), :]
                    for g in range(pieces):
                        turned = pltpu.roll(block, lax.rem(y + (LANES - g * SUB), LANES), 1)
                        old = out_ref[k, part, pl.ds(x + 8 * g, 8), :]
                        new.append(old + jnp.where(inside, turned, 0.0))
                for part in range(2):
                    for g in range(pieces):
                        out_ref[k, part, pl.ds(x + 8 * g, 8), :] = new[part * pieces + g]
                return carry

            lax.fori_loop(0, place_ref[t, 4, 0], add, 0)


def place_on_grid(places, blocks, factors, per_owner, capacity):
    groups, rows, depth = blocks.shape
    sources = rows // capacity
    width = 2 * LANES
    return pl.pallas_call(
        functools.partial(grid_kernel, sources, capacity),
        grid=(factors.shape[1] // width,),
        in_specs=[
            pl.BlockSpec(memory_space=pltpu.SMEM),
            pl.BlockSpec((groups, rows, depth), lambda i: (0, 0, 0)),
            pl.BlockSpec((factors.shape[0], width), lambda i: (0, i)),
        ],
        out_specs=pl.BlockSpec((per_owner, 2, TILE_SIDE, TILE_SIDE), lambda i: (0, 0, 0, 0)),
        out_shape=jax.ShapeDtypeStruct((per_owner, 2, TILE_SIDE, TILE_SIDE), jnp.float32),
        scratch_shapes=[pltpu.VMEM((rows * 2 * PIX // LANES, LANES), jnp.float32)],
        compiler_params=pltpu.CompilerParams(vmem_limit_bytes=VMEM_LIMIT),
        name="grid",
    )(places, blocks, factors)


def uv_factors():
    per_tile = LANES // SUB
    index = np.arange(SUB) - SUB // 2
    angle = -2.0 * np.pi / SUB * ((index[:, None] * index[None, :]) % SUB)
    factor = np.exp(1j * angle)
    both = (factor / SUB)[None, :, :, None] * factor[:, None, None, :]
    both = both.reshape(SUB // per_tile, per_tile, SUB, SUB // 8, 8, SUB).transpose(0, 1, 2, 4, 3, 5)
    table = np.empty((SUB // per_tile, 2, per_tile, SUB, 2, 8, SUB // 8, SUB))
    table[:, 0, :, :, 0] = both.real
    table[:, 0, :, :, 1] = both.imag
    table[:, 1, :, :, 0] = -both.imag
    table[:, 1, :, :, 1] = both.real
    return table.reshape(2 * PIX, 2 * PIX).astype(jnp.bfloat16)


def taper_table(scale):
    pos = (np.arange(SUB) - SUB / 2 + 0.5) / (SUB / 2)
    one = 1.0 - 0.8 * pos * pos
    return (one[:, None] * one[None, :] * scale).astype(np.float32)


def per_device(visibilities, coords, stations, tile_ids, offsets, screens):
    count, fields, nvis = visibilities.shape
    ncorr = fields // 2
    groups = lax.axis_size("corr")
    owners = lax.axis_size("tile")
    corr = lax.axis_index("corr")
    tile = lax.axis_index("tile")
    per_owner = NT // owners
    capacity = per_owner * groups * (2 * count // NT)
    local = PIX // groups
    halves = local // LANES

    meta = jnp.concatenate([tile_ids, offsets, stations], axis=1)
    every = lax.all_gather(meta, ("corr", "tile"), axis=0, tiled=True).reshape(groups, owners, count, 5)
    station_list = lax.dynamic_index_in_dim(every, tile, axis=1, keepdims=False)[..., 3:].reshape(groups * count, 2)
    by_row = jnp.transpose(every[..., :3], (3, 1, 0, 2)).reshape(3, owners, groups * count)
    all_tiles = by_row[0][:, None, :]
    all_offsets = jnp.transpose(by_row[1:], (1, 0, 2))
    my_tiles = lax.dynamic_index_in_dim(all_tiles, tile, axis=0, keepdims=False)

    part = lax.dynamic_slice_in_dim(screens, corr * local, local, axis=2)
    part = part.reshape(-1, fields, halves, LANES).transpose(0, 2, 1, 3).reshape(-1, fields * local)
    all_screens = lax.all_gather(part, "tile", axis=0, tiled=True)

    images = make_images(visibilities, coords, groups)
    images = lax.all_to_all(images, "corr", split_axis=0, concat_axis=0, tiled=True)
    images = images.reshape(groups * count, fields * local)

    taper = jnp.asarray(taper_table(1.0 / nvis)).reshape(groups, halves, 1, LANES)
    taper = lax.dynamic_index_in_dim(taper, corr, axis=0, keepdims=False)
    sending = apply_aterms(images, all_screens, station_list, my_tiles, taper, ncorr, owners, per_owner, capacity)
    received = lax.all_to_all(
        sending.reshape(groups * owners, capacity, 2 * local), ("corr", "tile"), split_axis=0, concat_axis=0, tiled=True
    )
    places = find_places(all_tiles, all_offsets, owners, per_owner, capacity)
    factors = jnp.asarray(uv_factors())
    grid = place_on_grid(places, received.reshape(groups, owners * capacity, 2 * local), factors, per_owner, capacity)
    return grid[None]


def solution(mesh):
    return jax.shard_map(
        per_device,
        mesh=mesh,
        in_specs=(
            P(("corr", "tile"), None, None),
            P(("corr", "tile"), None, None),
            P(("corr", "tile"), None),
            P(("corr", "tile"), None),
            P(("corr", "tile"), None),
            P("tile", None, None),
        ),
        out_specs=P("corr", "tile", None, None, None),
        check_vma=False,
    )
```

profile of v0, /device:TPU:19, one launch (start us, length us, event | category | flops | bytes accessed | tf_op | source)
XLA Modules:
  0.0 175.0 jit_solution(10889019234964445737)
XLA Ops:
  6.5 0.0 copy-start
  6.5 0.0 all-gather.3.cloned.1.call-start
  6.5 1.2 copy-done
  7.8 0.8 copy.19
  8.6 0.0 all-gather.3.cloned.1.call-update
  8.6 1.1 copy.14.coord_ref
  9.6 0.0 copy-start.2
  9.7 0.9 copy-done.2
  10.6 12.2 %images.1 = bf16[4,64,2048]{2,1,0:T(8,128)(2,1)} custom-call(bf16[64,8,256]{2,1,0:T(8,128)(2,1)S(1)} %copy-done.2, f32[64,3,256]{2,1,0:T(4,128)S(1)} %copy.14.coord_ref), custom_call_target="tpu_custom_call" | custom-call | flops 2147483648 | bytes 2097152 | tf_op jit(solution)/shard_map/images/pallas_call | solution.py:112
  22.8 3.9 %all-to-all-start = ((bf16[4,64,2048]{2,1,0:T(8,128)(2,1)}), bf16[4,64,2048]{2,1,0:T(8,128)(2,1)S(1)}, u32[]{:S(2)}, u32[]{:S(2)}) async-start(bf16[4,64,2048]{2,1,0:T(8,128)(2,1)} %images.1), calls=%async_computation | async-start | bytes 2097152 | tf_op jit(solution)/shard_map/all_to_all | solution.py:361
  26.7 0.0 copy-done.3
  26.7 36.0 %all-gather = s32[32,64,5]{1,2,0:T(8,128)S(1)} all-gather(s32[1,64,5]{1,2,0:T(8,128)S(1)} %add_bitcast_fusion), channel_id=1, replica_groups=mesh['corr'=4,'tile'=8] {'corr','tile'}, dimensions={0}, use_global_device_ids=true | all-gather | bytes 42240 | tf_op jit(solution)/shard_map/all_gather | solution.py:349
  62.8 0.1 broadcast_in_dim_squeeze.3.tiles_ref
  62.9 0.1 copy.13
  63.0 0.1 slice.24
  63.1 0.7 constant_dynamic-slice_fusion.1
  63.8 0.0 all-to-all-done
  63.8 1.6 copy-done.1
  65.4 5.3 %aterms.1 = bf16[4,512,512]{2,1,0:T(8,128)(2,1)} custom-call(s32[256,2]{1,0:T(8,128)S(1)} %bitcast.30, s32[1,256]{1,0:T(1,128)S(1)} %dynamic-slice_bitcast_fusion.tiles_ref, f32[2,1,128]{2,1,0:T(1,128)S(1)} %bitcast.32, bf16[256,2048]{1,0:T(8,128)(2,1)S(1)} %bitcast.29, bf16[512,2048]{1,0:T(8,128)(2,1)S(1)} %copy-done.1), custom_call_target="tpu_custom_call" | custom-call | tf_op jit(solution)/shard_map/aterms/pallas_call | solution.py:199
  70.7 10.1 %all-to-all-start.1 = ((bf16[32,64,512]{2,1,0:T(8,128)(2,1)}), bf16[32,64,512]{2,1,0:T(8,128)(2,1)S(1)}, u32[]{:S(2)}, u32[]{:S(2)}) async-start(bf16[32,64,512]{2,1,0:T(8,128)(2,1)} %bitcast.11), calls=%async_computation.1 | async-start | bytes 4194304 | tf_op jit(solution)/shard_map/all_to_all | solution.py:367
  80.8 0.1 slice.19
  80.9 1.5 places.1.place_ref
  82.3 44.6 %all-to-all-done.1 = bf16[32,64,512]{2,1,0:T(8,128)(2,1)S(1)} async-done(((bf16[32,64,512]{2,1,0:T(8,128)(2,1)}), bf16[32,64,512]{2,1,0:T(8,128)(2,1)S(1)}, u32[]{:S(2)}, u32[]{:S(2)}) %all-to-all-start.1) | async-done | bytes 2097184 | tf_op jit(solution)/shard_map/all_to_all | solution.py:367
  126.9 41.3 %grid.1 = f32[8,2,128,128]{3,2,1,0:T(8,128)} custom-call(s32[8,8,64]{2,1,0:T(8,128)S(1)} %places.1.place_ref, bf16[4,512,512]{2,1,0:T(8,128)(2,1)S(1)} %bitcast.28, bf16[2048,2048]{1,0:T(8,128)(2,1)} %constant.33.clone.factor_ref), custom_call_target="tpu_custom_call" | custom-call | tf_op jit(solution)/shard_map/grid/pallas_call | solution.py:299
  (15 shorter events, 0.1 us)
Async XLA Ops:
  6.5 1.2 copy-start
  6.5 57.3 %all-gather.3.cloned.1.call-start = ((), (), s32[]{:S(2)}) async-start(), calls=%async_computation.2 | async-start | bytes 2359296 | tf_op jit(solution)/shard_map/all_gather | solution.py:358
  9.6 1.0 copy-start.2
  22.8 3.9 %copy-start.3 = (s32[64,2]{0,1:T(2,128)S(1)}, s32[64,2]{0,1:T(2,128)}, u32[]{:S(2)}) copy-start(s32[64,2]{0,1:T(2,128)} %param.10) | copy-start | bytes 1540
  22.8 3.9 %copy-start.4 = (s32[64,2]{0,1:T(2,128)S(1)}, s32[64,2]{0,1:T(2,128)}, u32[]{:S(2)}) copy-start(s32[64,2]{0,1:T(2,128)} %param.12) | copy-start | bytes 1540
  22.8 3.9 %copy-start.5 = (s32[64,1]{0,1:T(1,128)S(1)}, s32[64,1]{0,1:T(1,128)}, u32[]{:S(2)}) copy-start(s32[64,1]{0,1:T(1,128)} %param.11) | copy-start | bytes 772
  22.8 41.0 %all-to-all-start = ((bf16[4,64,2048]{2,1,0:T(8,128)(2,1)}), bf16[4,64,2048]{2,1,0:T(8,128)(2,1)S(1)}, u32[]{:S(2)}, u32[]{:S(2)}) async-start(bf16[4,64,2048]{2,1,0:T(8,128)(2,1)} %images.1), calls=%async_computation | async-start | bytes 2097152 | tf_op jit(solution)/shard_map/all_to_all | solution.py:361
  63.8 1.6 copy-start.1
  70.7 56.3 %all-to-all-start.1 = ((bf16[32,64,512]{2,1,0:T(8,128)(2,1)}), bf16[32,64,512]{2,1,0:T(8,128)(2,1)S(1)}, u32[]{:S(2)}, u32[]{:S(2)}) async-start(bf16[32,64,512]{2,1,0:T(8,128)(2,1)} %bitcast.11), calls=%async_computation.1 | async-start | bytes 4194304 | tf_op jit(solution)/shard_map/all_to_all | solution.py:367
Sparse Core Ops, SparseCore 0:
  9.0 30.3 all-gather.2
where the time goes:
time: 174 us; the launch traced here: 175 us
  Pallas kernels  60.2 us (35%)
  waiting for transfers between devices  44.6 us (26%)
  blocking collectives  36 us (21%)
  starting transfers between devices  14 us (8%)
  between operations  13.5 us (8%)
  local copies, waits for them, and re-layouts  6.77 us (4%)
    all_to_all x1, waiting for transfers between devices, per_device(): lax.all_to_all(sending.reshape(groups * owners, capacity, 2 * local), ('c...  44.6 us
    pallas_call x1, Pallas kernels, place_on_grid(): pl.pallas_call(functools.partial(grid_kernel, sources, capacity), grid=(f...  41.3 us
    all_gather x1, blocking collectives, per_device(): lax.all_gather(meta, ('corr', 'tile'), axis=0, tiled=True)  36 us
    pallas_call x1, Pallas kernels, make_images(): pl.pallas_call(functools.partial(image_kernel, ncorr, groups), grid=(coun...  12.2 us
    all_to_all x1, starting transfers between devices, per_device(): lax.all_to_all(sending.reshape(groups * owners, capacity, 2 * local), ('c...  10.1 us
    unnamed x15, local copies, waits for them, and re-layouts  5.63 us
    pallas_call x1, Pallas kernels, apply_aterms(): pl.pallas_call(functools.partial(aterm_kernel, ncorr, owners, per_owner,...  5.27 us
    all_to_all x1, starting transfers between devices, per_device(): lax.all_to_all(images, 'corr', split_axis=0, concat_axis=0, tiled=True)  3.88 us
  transfers between devices with their start and end apart: 3, of which 1 were waited for; matrix products, arithmetic and copies ran while one was open for 1% of the time, Pallas kernels for 8%

commit v1 on v0

v1 whole, which is shorter than its diff:
```python
import functools
import math

import jax
import jax.numpy as jnp
import numpy as np
from jax import lax
from jax.experimental import pallas as pl
from jax.experimental.pallas import tpu as pltpu
from jax.sharding import PartitionSpec as P

SUB = 32
NT = 64
TILE_SIDE = 128
PIX = SUB * SUB
LANES = 128
VMEM_LIMIT = 48 * 1024 * 1024

ROOT2 = math.sqrt(2.0)


def half_turn_series():
    grid = np.cos(np.pi * (np.arange(400) + 0.5) / 800.0) * 0.5
    z = grid * grid
    sine = np.polynomial.polynomial.Polynomial.fit(z, np.sin(np.pi * grid) / grid, 4, domain=[0, 0.25], window=[0, 0.25]).coef
    cosine = np.polynomial.polynomial.Polynomial.fit(z, np.cos(np.pi * grid), 4, domain=[0, 0.25], window=[0, 0.25]).coef
    return [float(x) * ROOT2 for x in sine], [float(x) * ROOT2 for x in cosine]


SINE, COSINE = half_turn_series()


def horner(coefficients, z):
    total = coefficients[-1]
    for value in coefficients[-2::-1]:
        total = total * z + value
    return total


def cis_turns(turns):
    t = turns - jnp.round(turns)
    z = t * t
    s = t * horner(SINE, z)
    c = horner(COSINE, z)
    return 1.0 - s * s, s * c


def image_kernel(ncorr, groups, vis_ref, coord_ref, station_ref, tile_ref, offset_ref, out_ref, square):
    step = vis_ref.shape[0]
    nvis = vis_ref.shape[2]
    centred = (lax.broadcasted_iota(jnp.int32, (SUB, nvis), 0) - SUB // 2).astype(jnp.float32) * (1.0 / SUB)
    bend = 0.5 * centred * centred
    rows = ncorr * SUB

    def one(s):
        u = coord_ref[s, 0:1, :]
        v = coord_ref[s, 1:2, :]
        w = coord_ref[s, 2:3, :]
        sag = w * bend
        e_re, e_im = cis_turns(u * centred - sag)
        f_re, f_im = cis_turns(v * centred - sag)
        vis = vis_ref[s].astype(jnp.float32)
        g_re = []
        g_im = []
        for e in range(ncorr):
            vr = vis[e : e + 1]
            vi = vis[ncorr + e : ncorr + e + 1]
            g_re.append((vr * e_re - vi * e_im).astype(jnp.bfloat16))
            g_im.append((vr * e_im + vi * e_re).astype(jnp.bfloat16))
        left = jnp.concatenate([jnp.concatenate(g_re, axis=0), jnp.concatenate(g_im, axis=0)], axis=1)
        f_re = f_re.astype(jnp.bfloat16)
        f_im = f_im.astype(jnp.bfloat16)
        right = jnp.concatenate(
            [jnp.concatenate([f_re, f_im], axis=0), jnp.concatenate([-f_im, f_re], axis=0)], axis=1
        )
        image = lax.dot_general(left, right, (((1,), (1,)), ((), ())), preferred_element_type=jnp.float32)
        square[pl.ds(pl.multiple_of(s * rows, rows), rows), 0 : 2 * SUB] = image

    def several(i, carry):
        for j in range(4):
            one(i * 4 + j)
        return carry

    lax.fori_loop(0, step // 4, several, 0)

    lane = lax.broadcasted_iota(jnp.int32, (step, LANES), 1)
    per_tile = LANES // SUB
    halves = SUB // groups // per_tile
    for g in range(groups):
        for h in range(halves):
            for e in range(ncorr):
                real = None
                imag = None
                for j in range(per_tile):
                    r = (g * halves + h) * per_tile + j
                    piece = square[pl.ds(e * SUB + r, step, stride=rows), :]
                    a = piece if j == 0 else pltpu.roll(piece, SUB * j, 1)
                    b = piece if j == 1 else pltpu.roll(piece, (SUB * (j - 1)) % LANES, 1)
                    keep = lane < SUB * (j + 1)
                    real = a if real is None else jnp.where(lane < SUB * j, real, a)
                    imag = b if imag is None else jnp.where(lane < SUB * j, imag, b)
                base = h * 2 * ncorr * LANES
                out_ref[g, :, base + e * LANES : base + (e + 1) * LANES] = real.astype(jnp.bfloat16)
                out_ref[g, :, base + (ncorr + e) * LANES : base + (ncorr + e + 1) * LANES] = imag.astype(jnp.bfloat16)
    near = station_ref[:, 0:1]
    far = station_ref[:, 1:2]
    facts = (tile_ref[...], offset_ref[:, 0:1], offset_ref[:, 1:2], near // 256, near % 256, far // 256, far % 256)
    table = jnp.zeros((step, LANES), jnp.int32)
    for i, fact in enumerate(facts):
        table = jnp.where(lane == i, fact, table)
    table = table.astype(jnp.float32).astype(jnp.bfloat16)
    for g in range(groups):
        out_ref[g, :, 2 * ncorr * halves * LANES :] = table


def make_images(visibilities, coords, stations, tile_ids, offsets, groups):
    count, fields, nvis = visibilities.shape
    ncorr = fields // 2
    step = 16
    width = fields * PIX // groups + LANES
    return pl.pallas_call(
        functools.partial(image_kernel, ncorr, groups),
        grid=(count // step,),
        in_specs=[
            pl.BlockSpec((step, fields, nvis), lambda i: (i, 0, 0)),
            pl.BlockSpec((step, 3, nvis), lambda i: (i, 0, 0)),
            pl.BlockSpec((step, 2), lambda i: (i, 0)),
            pl.BlockSpec((step, 1), lambda i: (i, 0)),
            pl.BlockSpec((step, 2), lambda i: (i, 0)),
        ],
        out_specs=pl.BlockSpec((groups, step, width), lambda i: (0, i, 0)),
        out_shape=jax.ShapeDtypeStruct((groups, count, width), jnp.bfloat16),
        scratch_shapes=[pltpu.VMEM((step * ncorr * SUB, LANES), jnp.float32)],
        compiler_params=pltpu.CompilerParams(vmem_limit_bytes=VMEM_LIMIT),
        cost_estimate=pl.CostEstimate(flops=count * 2 * 128 * 512 * 256, bytes_accessed=2 << 20, transcendentals=0),
        name="images",
    )(visibilities, coords, stations, tile_ids, offsets)


def send_rows(owners, per_owner, window, half, facts, block_ref, out_ref):
    first, rows = window
    n = facts.shape[0]
    ncorr = out_ref.shape[0]
    slots = rows - 1
    turned = jnp.transpose(facts)
    owner = jnp.floor(turned[0:1] * (1.0 / per_owner))
    mine = lax.broadcasted_iota(jnp.int32, (owners, n), 0).astype(jnp.float32) == owner
    hot = mine.astype(jnp.float32)
    before = lax.broadcasted_iota(jnp.int32, (n, n), 0) < lax.broadcasted_iota(jnp.int32, (n, n), 1)
    ahead = jnp.dot(
        hot.astype(jnp.bfloat16), before.astype(jnp.float32).astype(jnp.bfloat16), preferred_element_type=jnp.float32
    )
    rank = jnp.sum(hot * ahead, axis=0, keepdims=True) - first
    fits = (rank >= 0.0) & (rank < float(slots))

    def chosen(pitch):
        place = jnp.where(fits, owner * pitch + rank, -1.0)
        row = lax.broadcasted_iota(jnp.int32, (owners * pitch, n), 0).astype(jnp.float32)
        return (row == place).astype(jnp.float32).astype(jnp.bfloat16)

    facts_here = jnp.concatenate(
        [turned[1:3], turned[0:1] - owner * per_owner, jnp.zeros((5, n), jnp.float32)], axis=0
    ).astype(jnp.bfloat16)
    found = lax.dot_general(facts_here, chosen(LANES), (((1,), (1,)), ((), ())), preferred_element_type=jnp.float32)
    held = jnp.sum(hot, axis=1, keepdims=True)
    most = jnp.max(held, axis=0, keepdims=True)
    here = jnp.minimum(jnp.maximum(held - first, 0.0), float(slots))
    lane = lax.broadcasted_iota(jnp.int32, (1, LANES), 1)
    labels = []
    for o in range(owners):
        span = slice(o * LANES, (o + 1) * LANES)
        counts = jnp.where(lane == 0, here[o : o + 1], jnp.where(lane == 1, most, 0.0))
        left = jnp.where(half == 0, found[0:1, span], found[2:3, span])
        right = jnp.where(half == 0, found[1:2, span], counts)
        labels.append(jnp.concatenate([left, right], axis=1))
    move = chosen(rows)
    last = lax.broadcasted_iota(jnp.int32, (16, 2 * LANES), 0) == 15
    for e in range(ncorr):
        moved = jnp.dot(move, block_ref[:, 2 * e * LANES : 2 * (e + 1) * LANES], preferred_element_type=jnp.float32)
        out_ref[e] = moved.astype(jnp.bfloat16)
        for o in range(owners):
            end = (o + 1) * rows
            out_ref[e, end - 16 : end, :] = jnp.where(last, labels[o], moved[end - 16 : end]).astype(jnp.bfloat16)


def aterm_kernel(ncorr, owners, per_owner, window, facts_ref, taper_ref, image_ref, screen_ref, out_ref, block_ref, near_ref, far_ref):
    n = image_ref.shape[0]
    nst = screen_ref.shape[0]
    facts = facts_ref[...].astype(jnp.float32)
    number = lax.broadcasted_iota(jnp.int32, (n, nst), 1).astype(jnp.float32)
    for column, ref in ((3, near_ref), (5, far_ref)):
        station = facts[:, column : column + 1] * 256.0 + facts[:, column + 1 : column + 2]
        pick = (number == station).astype(jnp.float32).astype(jnp.bfloat16)
        ref[...] = jnp.dot(pick, screen_ref[...], preferred_element_type=jnp.float32)
    taper = taper_ref[0]
    chunk = 16

    def part(ref, rows, field):
        return ref[rows, field * LANES : (field + 1) * LANES].astype(jnp.float32)

    def body(i, carry):
        rows = pl.ds(pl.multiple_of(i * chunk, chunk), chunk)
        image_re = [part(image_ref, rows, e) for e in range(ncorr)]
        image_im = [part(image_ref, rows, ncorr + e) for e in range(ncorr)]
        for row_out in range(2):
            mid_re = []
            mid_im = []
            for inner in range(2):
                m_re = 0.0
                m_im = 0.0
                for first in range(2):
                    near_re = part(near_ref, rows, 2 * first + row_out)
                    near_im = part(near_ref, rows, ncorr + 2 * first + row_out)
                    vis_re = image_re[2 * first + inner]
                    vis_im = image_im[2 * first + inner]
                    m_re = m_re + near_re * vis_re + near_im * vis_im
                    m_im = m_im + near_re * vis_im - near_im * vis_re
                mid_re.append(m_re)
                mid_im.append(m_im)
            for col_out in range(2):
                t_re = 0.0
                t_im = 0.0
                for inner in range(2):
                    far_re = part(far_ref, rows, 2 * inner + col_out)
                    far_im = part(far_ref, rows, ncorr + 2 * inner + col_out)
                    t_re = t_re + mid_re[inner] * far_re - mid_im[inner] * far_im
                    t_im = t_im + mid_re[inner] * far_im + mid_im[inner] * far_re
                place = 2 * (2 * row_out + col_out) * LANES
                block_ref[rows, place : place + LANES] = (t_re * taper).astype(jnp.bfloat16)
                block_ref[rows, place + LANES : place + 2 * LANES] = (t_im * taper).astype(jnp.bfloat16)
        return carry

    lax.fori_loop(0, n // chunk, body, 0)
    send_rows(owners, per_owner, window, pl.program_id(0), facts, block_ref, out_ref)


def apply_aterms(images, screens, taper, ncorr, owners, per_owner, window):
    n = images.shape[0]
    nst = screens.shape[0]
    half = 2 * ncorr * LANES
    halves = screens.shape[1] // half
    rows = owners * window[1]
    return pl.pallas_call(
        functools.partial(aterm_kernel, ncorr, owners, per_owner, window),
        grid=(halves,),
        in_specs=[
            pl.BlockSpec((n, LANES), lambda h: (0, halves * 2 * ncorr)),
            pl.BlockSpec((1, 1, LANES), lambda h: (h, 0, 0)),
            pl.BlockSpec((n, half), lambda h: (0, h)),
            pl.BlockSpec((nst, half), lambda h: (0, h)),
        ],
        out_specs=[
            pl.BlockSpec((ncorr, rows, 2 * LANES), lambda h: (0, 0, h)),
            pl.BlockSpec((n, half), lambda h: (0, h)),
        ],
        out_shape=[
            jax.ShapeDtypeStruct((ncorr, rows, halves * 2 * LANES), jnp.bfloat16),
            jax.ShapeDtypeStruct((n, halves * half), jnp.bfloat16),
        ],
        scratch_shapes=[pltpu.VMEM((n, half), jnp.float32), pltpu.VMEM((n, half), jnp.float32)],
        compiler_params=pltpu.CompilerParams(vmem_limit_bytes=VMEM_LIMIT),
        name="aterms",
    )(images, taper, images, screens)


def rest_kernel(owners, per_owner, window, facts_ref, block_ref, out_ref):
    send_rows(owners, per_owner, window, pl.program_id(0), facts_ref[...].astype(jnp.float32), block_ref, out_ref)


def send_rest(images, blocks, ncorr, owners, per_owner, window):
    n = images.shape[0]
    half = 2 * ncorr * LANES
    halves = blocks.shape[1] // half
    rows = owners * window[1]
    return pl.pallas_call(
        functools.partial(rest_kernel, owners, per_owner, window),
        grid=(halves,),
        in_specs=[
            pl.BlockSpec((n, LANES), lambda h: (0, halves * 2 * ncorr)),
            pl.BlockSpec((n, half), lambda h: (0, h)),
        ],
        out_specs=pl.BlockSpec((ncorr, rows, 2 * LANES), lambda h: (0, 0, h)),
        out_shape=jax.ShapeDtypeStruct((ncorr, rows, halves * 2 * LANES), jnp.bfloat16),
        compiler_params=pltpu.CompilerParams(vmem_limit_bytes=VMEM_LIMIT),
        name="rest",
    )(images, blocks)


def grid_kernel(rows, block_ref, col_ref, row_ref, before_ref, out_ref, most_ref, half_ref, uv_ref, turned_ref, re_a, im_a, re_b, im_b, label_ref, place_ref, sem):
    groups, total, depth = block_ref.shape
    sources = total // rows
    per_slot = 2 * PIX // LANES
    quarters = depth // LANES
    for t in range(sources):
        end = (t + 1) * rows
        label_ref[t : t + 1, :] = block_ref[0, end - 16 : end, :].astype(jnp.float32)[15:16].astype(jnp.int32)
    fetch = pltpu.make_async_copy(label_ref, place_ref, sem)
    fetch.start()

    for g in range(groups):
        half_ref[g] = jnp.dot(block_ref[g], col_ref[...], preferred_element_type=jnp.float32).astype(jnp.bfloat16)
    for q in range(quarters):
        left = jnp.concatenate([half_ref[g, :, q * LANES : (q + 1) * LANES] for g in range(groups)], axis=1)
        uv = jnp.dot(left, row_ref[...], preferred_element_type=jnp.float32)
        for part in range(2):
            for i in range(2):
                j = part * 2 + i
                uv_ref[pl.ds(part * 8 + 2 * q + i, total, stride=per_slot), :] = uv[:, j * LANES : (j + 1) * LANES]
    for t in range(sources):
        uv_ref[((t + 1) * rows - 1) * per_slot : (t + 1) * rows * per_slot, :] = jnp.zeros((per_slot, LANES), jnp.float32)
    for ref in (re_a, im_a, re_b, im_b):
        ref[...] = jnp.zeros_like(ref)
    fetch.wait()

    lane = lax.broadcasted_iota(jnp.int32, (8, LANES), 1)
    pieces = LANES // SUB
    tall = 2 * pieces * 8
    batch = 8
    most = jnp.int32(0)
    for t in range(sources):
        count = place_ref[t, 3 * LANES]
        most = jnp.maximum(most, place_ref[t, 3 * LANES + 1])

        def turn(i, carry):
            for b in range(batch):
                j = i * batch + b
                y = place_ref[t, LANES + j]
                inside = (lane >= y) & (lane < y + SUB)
                slot = t * rows + j
                for part in range(2):
                    block = uv_ref[pl.ds(pl.multiple_of(slot * per_slot + part * 8, 8), 8), :]
                    for g in range(pieces):
                        moved = pltpu.roll(block, (y + (LANES - g * SUB)) & (LANES - 1), 1)
                        at = pl.multiple_of(slot * tall + (part * pieces + g) * 8, 8)
                        turned_ref[pl.ds(at, 8), :] = jnp.where(inside, moved, 0.0)
            return carry

        lax.fori_loop(0, (count + (batch - 1)) // batch, turn, 0)

        def add(i, carry):
            for b in range(4):
                j = i * 4 + b
                row = place_ref[t, 2 * LANES + j] * TILE_SIDE + place_ref[t, j]
                slot = t * rows + j
                for part, ref in enumerate((re_a, im_a) if b % 2 == 0 else (re_b, im_b)):
                    at = pl.multiple_of(slot * tall + part * pieces * 8, 8)
                    ref[pl.ds(row, SUB), :] = ref[pl.ds(row, SUB), :] + turned_ref[pl.ds(at, SUB), :]
            return carry

        lax.fori_loop(0, (count + 3) // 4, add, 0)

    most_ref[0] = most
    for k in range(out_ref.shape[0]):
        span = slice(k * TILE_SIDE, (k + 1) * TILE_SIDE)
        for part, (one, two) in enumerate(((re_a, re_b), (im_a, im_b))):
            value = one[span, :] + two[span, :]
            if before_ref is not None:
                value = value + before_ref[k, part]
            out_ref[k, part] = value


def first_grid_kernel(rows, block_ref, col_ref, row_ref, *refs):
    grid_kernel(rows, block_ref, col_ref, row_ref, None, *refs)


def place_on_grid(blocks, rows, tables, per_owner, before=None):
    groups, total, depth = blocks.shape
    sources = total // rows
    shape = (per_owner, 2, TILE_SIDE, TILE_SIDE)
    whole = pl.BlockSpec(memory_space=pltpu.VMEM)
    accumulator = pltpu.VMEM((per_owner * TILE_SIDE, TILE_SIDE), jnp.float32)
    given = (blocks,) + tables + (() if before is None else (before,))
    return pl.pallas_call(
        functools.partial(first_grid_kernel if before is None else grid_kernel, rows),
        in_specs=[whole] * len(given),
        out_specs=[whole, pl.BlockSpec(memory_space=pltpu.SMEM)],
        out_shape=[jax.ShapeDtypeStruct(shape, jnp.float32), jax.ShapeDtypeStruct((1,), jnp.int32)],
        scratch_shapes=[
            pltpu.VMEM((groups, total, depth), jnp.bfloat16),
            pltpu.VMEM((total * 2 * PIX // LANES, LANES), jnp.float32),
            pltpu.VMEM((total * 2 * PIX // SUB, LANES), jnp.float32),
            accumulator,
            accumulator,
            accumulator,
            accumulator,
            pltpu.VMEM((sources, depth), jnp.int32),
            pltpu.SMEM((sources, depth), jnp.int32),
            pltpu.SemaphoreType.DMA(()),
        ],
        compiler_params=pltpu.CompilerParams(vmem_limit_bytes=VMEM_LIMIT),
        name="grid",
    )(*given)


def uv_tables(groups):
    quad = LANES // SUB
    halves = SUB // (groups * quad)
    index = np.arange(SUB) - SUB // 2
    factor = np.exp(-2j * np.pi / SUB * ((index[:, None] * index[None, :]) % SUB))

    def parts(table, axis):
        upper = np.stack([table.real, table.imag], axis=axis)
        lower = np.stack([-table.imag, table.real], axis=axis)
        return upper, lower

    col = (factor / SUB).reshape(SUB, 4, 4, 2).transpose(2, 0, 3, 1)
    first = np.zeros((halves, 2, quad, SUB, 4, halves, 2, quad, 2, 4))
    for p, table in enumerate(parts(col, 0)):
        for h in range(halves):
            for r in range(quad):
                first[h, p, r, :, :, h, :, r] = table.transpose(2, 1, 0, 3, 4)
    second = np.zeros((groups, halves, 2, quad, 2, 4, 2, 2, 4, SUB))
    row = factor.reshape(groups, halves, quad, SUB)
    for p, table in enumerate(parts(row, 0)):
        for i in range(2):
            for g in range(4):
                second[:, :, p, :, i, g, :, i, g, :] = table.transpose(1, 2, 3, 0, 4)
    size = halves * 2 * LANES
    first = first.reshape(size, 4 * halves * 2 * quad * 8)
    second = second.reshape(groups * halves * 2 * quad * 8, 4 * LANES)
    return first.astype(jnp.bfloat16), second.astype(jnp.bfloat16)


def taper_table(scale):
    pos = (np.arange(SUB) - SUB / 2 + 0.5) / (SUB / 2)
    one = 1.0 - 0.8 * pos * pos
    return (one[:, None] * one[None, :] * scale).astype(np.float32)


def per_device(visibilities, coords, stations, tile_ids, offsets, screens):
    count, fields, nvis = visibilities.shape
    ncorr = fields // 2
    groups = lax.axis_size("corr")
    owners = lax.axis_size("tile")
    corr = lax.axis_index("corr")
    tile = lax.axis_index("tile")
    per_owner = NT // owners
    full = per_owner * groups * (2 * count // NT)
    rows = -(-full * 3 // 64) * 16
    local = PIX // groups
    halves = local // LANES

    part = lax.dynamic_slice_in_dim(screens, corr * local, local, axis=2)
    part = part.reshape(-1, fields, halves, LANES).transpose(0, 2, 1, 3).reshape(-1, fields * local)
    all_screens = lax.all_gather(part, "tile", axis=0, tiled=True)

    images = make_images(visibilities, coords, stations, tile_ids, offsets, groups)
    images = lax.all_to_all(images, "corr", split_axis=0, concat_axis=0, tiled=True)
    images = images.reshape(groups * count, -1)

    taper = jnp.asarray(taper_table(1.0 / nvis)).reshape(groups, halves, 1, LANES)
    taper = lax.dynamic_index_in_dim(taper, corr, axis=0, keepdims=False)
    tables = tuple(jnp.asarray(table) for table in uv_tables(groups))

    def exchange(sending, rows):
        received = lax.all_to_all(
            sending.reshape(groups * owners, rows, 2 * local), ("corr", "tile"), split_axis=0, concat_axis=0, tiled=True
        )
        return received.reshape(groups, owners * rows, 2 * local)

    sending, blocks = apply_aterms(images, all_screens, taper, ncorr, owners, per_owner, (0, rows))
    grid, most = place_on_grid(exchange(sending, rows), rows, tables, per_owner)
    slots = rows - 1
    if slots < full:
        more = -(-(full - slots + 1) // 16) * 16

        def overflow(grid):
            rest = send_rest(images, blocks, ncorr, owners, per_owner, (slots, more))
            return place_on_grid(exchange(rest, more), more, tables, per_owner, grid)[0]

        grid = lax.cond(most[0] > slots, overflow, lambda grid: grid, grid)
    return grid[None]


def solution(mesh):
    return jax.shard_map(
        per_device,
        mesh=mesh,
        in_specs=(
            P(("corr", "tile"), None, None),
            P(("corr", "tile"), None, None),
            P(("corr", "tile"), None),
            P(("corr", "tile"), None),
            P(("corr", "tile"), None),
            P("tile", None, None),
        ),
        out_specs=P("corr", "tile", None, None, None),
        check_vma=False,
    )
```

time: 174 us -> 113 us (0.65)
  the two profiles are of different devices: /device:TPU:19 before, /device:TPU:0 now
where the time goes in v1:
time: 113 us; the launch traced here: 112 us
  blocking collectives  43.6 us (39%)
  Pallas kernels  27.1 us (24%)
  between operations  14.2 us (13%)
  waiting for transfers between devices  13.7 us (12%)
  local copies, waits for them, and re-layouts  7.93 us (7%)
  starting transfers between devices  5.16 us (5%)
    all_to_all x1, blocking collectives, exchange(): lax.all_to_all(sending.reshape(groups * owners, rows, 2 * local), ('corr'...  43.6 us
    all_to_all x1, waiting for transfers between devices, per_device(): lax.all_to_all(images, 'corr', split_axis=0, concat_axis=0, tiled=True)  13.7 us
    pallas_call x1, Pallas kernels, make_images(): pl.pallas_call(functools.partial(image_kernel, ncorr, groups), grid=(coun...  12.2 us
    pallas_call x1, Pallas kernels, place_on_grid(): pl.pallas_call(functools.partial(first_grid_kernel if before is None else...  9.84 us
    unnamed x18, local copies, waits for them, and re-layouts  7.21 us
    all_to_all x1, starting transfers between devices, per_device(): lax.all_to_all(images, 'corr', split_axis=0, concat_axis=0, tiled=True)  5.16 us
    pallas_call x1, Pallas kernels, apply_aterms(): pl.pallas_call(functools.partial(aterm_kernel, ncorr, owners, per_owner,...  5.04 us
  transfers between devices with their start and end apart: 2, of which 1 were waited for; matrix products, arithmetic and copies ran while one was open for 4% of the time, Pallas kernels for 11%

profile of v1, /device:TPU:0, one launch (start us, length us, event | category | flops | bytes accessed | tf_op | source)
XLA Modules:
  0.0 111.6 jit_solution(2370386090964966074)
XLA Ops:
  6.5 0.0 copy-start
  6.5 0.0 all-gather.2.cloned.1.call-start
  6.5 1.2 %copy-done = bf16[64,8,1024]{2,1,0:T(8,128)(2,1)S(1)} copy-done((bf16[64,8,1024]{2,1,0:T(8,128)(2,1)S(1)}, bf16[64,8,1024]{2,1,0:T(8,128)(2,1)}, u32[]{:S(2)}) %copy-start) | copy-done | bytes 1048600
  7.8 0.8 copy.18
  8.6 0.0 all-gather.2.cloned.1.call-update
  8.6 0.8 copy.13.station_ref
  9.4 0.7 copy.14.tile_ref
  10.1 0.8 copy.15.offset_ref
  10.9 1.1 copy.12.coord_ref
  11.9 0.0 copy-done.2
  12.0 12.2 %images.1 = bf16[4,64,2176]{2,1,0:T(8,128)(2,1)} custom-call(bf16[64,8,256]{2,1,0:T(8,128)(2,1)S(1)} %copy-done.2, f32[64,3,256]{2,1,0:T(4,128)S(1)} %copy.12.coord_ref, s32[64,2]{1,0:T(8,128)S(1)} %copy.13.station_ref, s32[64,1]{1,0:T(8,128)S(1)} %copy.14.tile_ref, s32[64,2]{1,0:T(8,128)S(1)} %copy.15.offset_ref), custom_call_target="tpu_custom_call" | custom-call | flops 2147483648 | bytes 2097152 | tf_op jit(solution)/shard_map/images/pallas_call | solution.py:121
  24.2 5.2 %all-to-all-start.1 = ((bf16[4,64,2176]{2,1,0:T(8,128)(2,1)}), bf16[4,64,2176]{2,1,0:T(8,128)(2,1)S(1)}, u32[]{:S(2)}, u32[]{:S(2)}) async-start(bf16[4,64,2176]{2,1,0:T(8,128)(2,1)} %images.1), calls=%async_computation.1 | async-start | bytes 2228224 | tf_op jit(solution)/shard_map/all_to_all | solution.py:448
  29.4 0.7 constant_dynamic-slice_fusion.1
  30.0 13.7 %all-to-all-done.1 = bf16[4,64,2176]{2,1,0:T(8,128)(2,1)S(1)} async-done(((bf16[4,64,2176]{2,1,0:T(8,128)(2,1)}), bf16[4,64,2176]{2,1,0:T(8,128)(2,1)S(1)}, u32[]{:S(2)}, u32[]{:S(2)}) %all-to-all-start.1) | async-done | bytes 1114144 | tf_op jit(solution)/shard_map/all_to_all | solution.py:448
  43.7 1.6 %copy-done.1 = bf16[512,2048]{1,0:T(8,128)(2,1)S(1)} copy-done((bf16[512,2048]{1,0:T(8,128)(2,1)S(1)}, bf16[512,2048]{1,0:T(8,128)(2,1)}, u32[]{:S(2)}) %copy-start.1) | copy-done | bytes 2097176
  45.3 5.0 %aterms.1 = (bf16[4,384,512]{2,1,0:T(8,128)(2,1)S(1)}, bf16[256,2048]{1,0:T(8,128)(2,1)S(1)}) custom-call(bf16[256,2176]{1,0:T(8,128)(2,1)S(1)} %bitcast.21, f32[2,1,128]{2,1,0:T(1,128)S(1)} %bitcast.20, bf16[256,2176]{1,0:T(8,128)(2,1)S(1)} %bitcast.22, bf16[512,2048]{1,0:T(8,128)(2,1)S(1)} %copy-done.1), custom_call_target="tpu_custom_call" | custom-call | tf_op jit(solution)/shard_map/aterms/pallas_call | solution.py:243
  50.3 0.0 copy-start.3
  50.4 0.0 copy-start.5
  50.4 43.6 %all_to_all.14 = bf16[32,48,512]{2,1,0:T(8,128)(2,1)S(1)} all-to-all(bf16[32,48,512]{2,1,0:T(8,128)(2,1)S(1)} %bitcast.19), channel_id=1, replica_groups=mesh['corr'=4,'tile'=8] {'corr','tile'}, dimensions={0} | all-to-all | bytes 3145728 | tf_op jit(solution)/shard_map/all_to_all | solution.py:456
  93.9 0.0 copy-done.3
  93.9 9.8 %grid.3 = (f32[8,2,128,128]{3,2,1,0:T(8,128)S(1)}, s32[1]{0:T(128)}) custom-call(bf16[4,384,512]{2,1,0:T(8,128)(2,1)S(1)} %bitcast.17, bf16[512,512]{1,0:T(8,128)(2,1)S(1)} %copy-done.5, bf16[512,512]{1,0:T(8,128)(2,1)S(1)} %copy-done.3), custom_call_target="tpu_custom_call" | custom-call | tf_op jit(solution)/shard_map/grid/pallas_call | solution.py:373
  103.8 0.0 copy-start.7
  104.5 0.1 copy.23
  104.6 0.2 copy-done.7
  (6 shorter events, 0.0 us)
Async XLA Ops:
  6.5 1.2 %copy-start = (bf16[64,8,1024]{2,1,0:T(8,128)(2,1)S(1)}, bf16[64,8,1024]{2,1,0:T(8,128)(2,1)}, u32[]{:S(2)}) copy-start(bf16[64,8,1024]{2,1,0:T(8,128)(2,1)} %param.16) | copy-start | bytes 3145732
  6.5 5.4 %copy-start.2 = (bf16[64,8,256]{2,1,0:T(8,128)(2,1)S(1)}, bf16[64,8,256]{2,1,0:T(8,128)(2,1)}, u32[]{:S(2)}) copy-start(bf16[64,8,256]{2,1,0:T(8,128)(2,1)} %vis_ref.1) | copy-start | bytes 786436
  6.5 37.2 %all-gather.2.cloned.1.call-start = ((), (), s32[]{:S(2)}) async-start(), calls=%async_computation.3 | async-start | bytes 2359296 | tf_op jit(solution)/shard_map/all_gather | solution.py:445
  24.2 19.5 %all-to-all-start.1 = ((bf16[4,64,2176]{2,1,0:T(8,128)(2,1)}), bf16[4,64,2176]{2,1,0:T(8,128)(2,1)S(1)}, u32[]{:S(2)}, u32[]{:S(2)}) async-start(bf16[4,64,2176]{2,1,0:T(8,128)(2,1)} %images.1), calls=%async_computation.1 | async-start | bytes 2228224 | tf_op jit(solution)/shard_map/all_to_all | solution.py:448
  43.7 1.6 %copy-start.1 = (bf16[512,2048]{1,0:T(8,128)(2,1)S(1)}, bf16[512,2048]{1,0:T(8,128)(2,1)}, u32[]{:S(2)}) copy-start(bf16[512,2048]{1,0:T(8,128)(2,1)} %all-gather.2.cloned.1.call-done.screen_ref) | copy-start | bytes 6291460
  50.3 43.6 %copy-start.3 = (bf16[512,512]{1,0:T(8,128)(2,1)S(1)}, bf16[512,512]{1,0:T(8,128)(2,1)}, u32[]{:S(2)}) copy-start(bf16[512,512]{1,0:T(8,128)(2,1)} %constant.27.clone.row_ref) | copy-start | bytes 1572868
  50.4 43.6 %copy-start.5 = (bf16[512,512]{1,0:T(8,128)(2,1)S(1)}, bf16[512,512]{1,0:T(8,128)(2,1)}, u32[]{:S(2)}) copy-start(bf16[512,512]{1,0:T(8,128)(2,1)} %constant.26.clone.col_ref) | copy-start | bytes 1572868
  103.8 1.0 copy-start.7
Sparse Core Ops, SparseCore 0:
  9.0 31.7 all-gather.1

commit v2 on v1

--- a/solution.py
+++ b/solution.py
@@ -45,7 +45,8 @@
     return 1.0 - s * s, s * c
 
 
-def image_kernel(ncorr, groups, vis_ref, coord_ref, station_ref, tile_ref, offset_ref, out_ref, square):
+def image_kernel(ncorr, groups, vis_ref, coord_ref, station_ref, tile_ref, offset_ref, *refs):
+    out_refs, square = refs[:-1], refs[-1]
     step = vis_ref.shape[0]
     nvis = vis_ref.shape[2]
     centred = (lax.broadcasted_iota(jnp.int32, (SUB, nvis), 0) - SUB // 2).astype(jnp.float32) * (1.0 / SUB)
@@ -53,9 +54,9 @@
     rows = ncorr * SUB
 
     def one(s):
-        u = coord_ref[s, 0:1, :]
-        v = coord_ref[s, 1:2, :]
-        w = coord_ref[s, 2:3, :]
+        u = coord_ref[0, pl.ds(s, 1), :]
+        v = coord_ref[1, pl.ds(s, 1), :]
+        w = coord_ref[2, pl.ds(s, 1), :]
         sag = w * bend
         e_re, e_im = cis_turns(u * centred - sag)
         f_re, f_im = cis_turns(v * centred - sag)
@@ -99,42 +100,47 @@
                     keep = lane < SUB * (j + 1)
                     real = a if real is None else jnp.where(lane < SUB * j, real, a)
                     imag = b if imag is None else jnp.where(lane < SUB * j, imag, b)
-                base = h * 2 * ncorr * LANES
-                out_ref[g, :, base + e * LANES : base + (e + 1) * LANES] = real.astype(jnp.bfloat16)
-                out_ref[g, :, base + (ncorr + e) * LANES : base + (ncorr + e + 1) * LANES] = imag.astype(jnp.bfloat16)
-    near = station_ref[:, 0:1]
-    far = station_ref[:, 1:2]
-    facts = (tile_ref[...], offset_ref[:, 0:1], offset_ref[:, 1:2], near // 256, near % 256, far // 256, far % 256)
-    table = jnp.zeros((step, LANES), jnp.int32)
+                out_refs[h][g, :, e * LANES : (e + 1) * LANES] = real.astype(jnp.bfloat16)
+                out_refs[h][g, :, (ncorr + e) * LANES : (ncorr + e + 1) * LANES] = imag.astype(jnp.bfloat16)
+    near = station_ref[0:1]
+    far = station_ref[1:2]
+    facts = (tile_ref[...], offset_ref[0:1], offset_ref[1:2], near // 256, near % 256, far // 256, far % 256)
+    count = near.shape[1]
+    field = lax.broadcasted_iota(jnp.int32, (LANES, count), 0)
+    table = jnp.zeros((LANES, count), jnp.int32)
     for i, fact in enumerate(facts):
-        table = jnp.where(lane == i, fact, table)
+        table = jnp.where(field == i, fact, table)
+    mine = lax.broadcasted_iota(jnp.int32, (step, count), 0) + pl.program_id(0) * step
+    mine = (mine == lax.broadcasted_iota(jnp.int32, (step, count), 1)).astype(jnp.float32).astype(jnp.bfloat16)
     table = table.astype(jnp.float32).astype(jnp.bfloat16)
+    table = lax.dot_general(mine, table, (((1,), (1,)), ((), ())), preferred_element_type=jnp.float32)
     for g in range(groups):
-        out_ref[g, :, 2 * ncorr * halves * LANES :] = table
+        out_refs[0][g, :, 2 * ncorr * LANES :] = table.astype(jnp.bfloat16)
 
 
 def make_images(visibilities, coords, stations, tile_ids, offsets, groups):
     count, fields, nvis = visibilities.shape
     ncorr = fields // 2
     step = 16
-    width = fields * PIX // groups + LANES
+    halves = PIX // (groups * LANES)
+    widths = [fields * LANES + (LANES if h == 0 else 0) for h in range(halves)]
     return pl.pallas_call(
         functools.partial(image_kernel, ncorr, groups),
         grid=(count // step,),
         in_specs=[
             pl.BlockSpec((step, fields, nvis), lambda i: (i, 0, 0)),
-            pl.BlockSpec((step, 3, nvis), lambda i: (i, 0, 0)),
-            pl.BlockSpec((step, 2), lambda i: (i, 0)),
-            pl.BlockSpec((step, 1), lambda i: (i, 0)),
-            pl.BlockSpec((step, 2), lambda i: (i, 0)),
+            pl.BlockSpec((3, step, nvis), lambda i: (0, i, 0)),
+            pl.BlockSpec((2, count), lambda i: (0, 0)),
+            pl.BlockSpec((1, count), lambda i: (0, 0)),
+            pl.BlockSpec((2, count), lambda i: (0, 0)),
         ],
-        out_specs=pl.BlockSpec((groups, step, width), lambda i: (0, i, 0)),
-        out_shape=jax.ShapeDtypeStruct((groups, count, width), jnp.bfloat16),
+        out_specs=[pl.BlockSpec((groups, step, width), lambda i: (0, i, 0)) for width in widths],
+        out_shape=[jax.ShapeDtypeStruct((groups, count, width), jnp.bfloat16) for width in widths],
         scratch_shapes=[pltpu.VMEM((step * ncorr * SUB, LANES), jnp.float32)],
         compiler_params=pltpu.CompilerParams(vmem_limit_bytes=VMEM_LIMIT),
-        cost_estimate=pl.CostEstimate(flops=count * 2 * 128 * 512 * 256, bytes_accessed=2 << 20, transcendentals=0),
+        cost_estimate=pl.CostEstimate(flops=count << 27, bytes_accessed=2 << 20, transcendentals=0),
         name="images",
-    )(visibilities, coords, stations, tile_ids, offsets)
+    )(visibilities, jnp.transpose(coords, (1, 0, 2)), stations.T, tile_ids.T, offsets.T)
 
 
 def send_rows(owners, per_owner, window, half, facts, block_ref, out_ref):
@@ -170,9 +176,8 @@
     for o in range(owners):
         span = slice(o * LANES, (o + 1) * LANES)
         counts = jnp.where(lane == 0, here[o : o + 1], jnp.where(lane == 1, most, 0.0))
-        left = jnp.where(half == 0, found[0:1, span], found[2:3, span])
-        right = jnp.where(half == 0, found[1:2, span], counts)
-        labels.append(jnp.concatenate([left, right], axis=1))
+        both = [found[0:1, span], found[1:2, span]] if half == 0 else [found[2:3, span], counts]
+        labels.append(jnp.concatenate(both, axis=1))
     move = chosen(rows)
     last = lax.broadcasted_iota(jnp.int32, (16, 2 * LANES), 0) == 15
     for e in range(ncorr):
@@ -183,7 +188,7 @@
             out_ref[e, end - 16 : end, :] = jnp.where(last, labels[o], moved[end - 16 : end]).astype(jnp.bfloat16)
 
 
-def aterm_kernel(ncorr, owners, per_owner, window, facts_ref, taper_ref, image_ref, screen_ref, out_ref, block_ref, near_ref, far_ref):
+def aterm_kernel(ncorr, owners, per_owner, window, half, facts_ref, taper_ref, image_ref, screen_ref, out_ref, block_ref, near_ref, far_ref):
     n = image_ref.shape[0]
     nst = screen_ref.shape[0]
     facts = facts_ref[...].astype(jnp.float32)
@@ -192,7 +197,7 @@
         station = facts[:, column : column + 1] * 256.0 + facts[:, column + 1 : column + 2]
         pick = (number == station).astype(jnp.float32).astype(jnp.bfloat16)
         ref[...] = jnp.dot(pick, screen_ref[...], preferred_element_type=jnp.float32)
-    taper = taper_ref[0]
+    taper = taper_ref[...]
     chunk = 16
 
     def part(ref, rows, field):
@@ -231,74 +236,88 @@
         return carry
 
     lax.fori_loop(0, n // chunk, body, 0)
-    send_rows(owners, per_owner, window, pl.program_id(0), facts, block_ref, out_ref)
-
-
-def apply_aterms(images, screens, taper, ncorr, owners, per_owner, window):
+    send_rows(owners, per_owner, window, half, facts, block_ref, out_ref)
+
+
+def apply_aterms(facts, images, screens, taper, ncorr, owners, per_owner, window, half):
     n = images.shape[0]
-    nst = screens.shape[0]
-    half = 2 * ncorr * LANES
-    halves = screens.shape[1] // half
+    nst, width = screens.shape
+    rows = owners * window[1]
+    whole = lambda shape: pl.BlockSpec(shape, lambda i: (0, 0))
+    return pl.pallas_call(
+        functools.partial(aterm_kernel, ncorr, owners, per_owner, window, half),
+        grid=(1,),
+        in_specs=[
+            pl.BlockSpec((n, LANES), lambda i: (0, 2 * ncorr)),
+            whole((1, LANES)),
+            whole((n, width)),
+            whole((nst, width)),
+        ],
+        out_specs=[pl.BlockSpec((ncorr, rows, 2 * LANES), lambda i: (0, 0, 0)), whole((n, width))],
+        out_shape=[
+            jax.ShapeDtypeStruct((ncorr, rows, 2 * LANES), jnp.bfloat16),
+            jax.ShapeDtypeStruct((n, width), jnp.bfloat16),
+        ],
+        scratch_shapes=[pltpu.VMEM((n, width), jnp.float32), pltpu.VMEM((n, width), jnp.float32)],
+        compiler_params=pltpu.CompilerParams(vmem_limit_bytes=VMEM_LIMIT),
+        cost_estimate=pl.CostEstimate(flops=3 << 30, bytes_accessed=4 << 20, transcendentals=0),
+        name="aterms",
+    )(facts, taper, images, screens)
+
+
+def rest_kernel(owners, per_owner, window, half, facts_ref, block_ref, out_ref):
+    send_rows(owners, per_owner, window, half, facts_ref[...].astype(jnp.float32), block_ref, out_ref)
+
+
+def send_rest(facts, block, ncorr, owners, per_owner, window, half):
+    n, width = block.shape
     rows = owners * window[1]
     return pl.pallas_call(
-        functools.partial(aterm_kernel, ncorr, owners, per_owner, window),
-        grid=(halves,),
+        functools.partial(rest_kernel, owners, per_owner, window, half),
+        grid=(1,),
         in_specs=[
-            pl.BlockSpec((n, LANES), lambda h: (0, halves * 2 * ncorr)),
-            pl.BlockSpec((1, 1, LANES), lambda h: (h, 0, 0)),
-            pl.BlockSpec((n, half), lambda h: (0, h)),
-            pl.BlockSpec((nst, half), lambda h: (0, h)),
+            pl.BlockSpec((n, LANES), lambda i: (0, 2 * ncorr)),
+            pl.BlockSpec((n, width), lambda i: (0, 0)),
         ],
-        out_specs=[
-            pl.BlockSpec((ncorr, rows, 2 * LANES), lambda h: (0, 0, h)),
-            pl.BlockSpec((n, half), lambda h: (0, h)),
-        ],
-        out_shape=[
-            jax.ShapeDtypeStruct((ncorr, rows, halves * 2 * LANES), jnp.bfloat16),
-            jax.ShapeDtypeStruct((n, halves * half), jnp.bfloat16),
-        ],
-        scratch_shapes=[pltpu.VMEM((n, half), jnp.float32), pltpu.VMEM((n, half), jnp.float32)],
-        compiler_params=pltpu.CompilerParams(vmem_limit_bytes=VMEM_LIMIT),
-        name="aterms",
-    )(images, taper, images, screens)
-
-
-def rest_kernel(owners, per_owner, window, facts_ref, block_ref, out_ref):
-    send_rows(owners, per_owner, window, pl.program_id(0), facts_ref[...].astype(jnp.float32), block_ref, out_ref)
-
-
-def send_rest(images, blocks, ncorr, owners, per_owner, window):
-    n = images.shape[0]
-    half = 2 * ncorr * LANES
-    halves = blocks.shape[1] // half
-    rows = owners * window[1]
-    return pl.pallas_call(
-        functools.partial(rest_kernel, owners, per_owner, window),
-        grid=(halves,),
-        in_specs=[
-            pl.BlockSpec((n, LANES), lambda h: (0, halves * 2 * ncorr)),
-            pl.BlockSpec((n, half), lambda h: (0, h)),
-        ],
-        out_specs=pl.BlockSpec((ncorr, rows, 2 * LANES), lambda h: (0, 0, h)),
-        out_shape=jax.ShapeDtypeStruct((ncorr, rows, halves * 2 * LANES), jnp.bfloat16),
+        out_specs=pl.BlockSpec((ncorr, rows, 2 * LANES), lambda i: (0, 0, 0)),
+        out_shape=jax.ShapeDtypeStruct((ncorr, rows, 2 * LANES), jnp.bfloat16),
         compiler_params=pltpu.CompilerParams(vmem_limit_bytes=VMEM_LIMIT),
         name="rest",
-    )(images, blocks)
-
-
-def grid_kernel(rows, block_ref, col_ref, row_ref, before_ref, out_ref, most_ref, half_ref, uv_ref, turned_ref, re_a, im_a, re_b, im_b, label_ref, place_ref, sem):
-    groups, total, depth = block_ref.shape
+    )(facts, block)
+
+
+def column_kernel(block_ref, col_ref, out_ref):
+    for g in range(block_ref.shape[0]):
+        out_ref[g] = jnp.dot(block_ref[g], col_ref[...], preferred_element_type=jnp.float32).astype(jnp.bfloat16)
+
+
+def transform_columns(blocks, table):
+    groups, total, depth = blocks.shape
+    return pl.pallas_call(
+        column_kernel,
+        out_shape=jax.ShapeDtypeStruct((groups, total, table.shape[1]), jnp.bfloat16),
+        compiler_params=pltpu.CompilerParams(vmem_limit_bytes=VMEM_LIMIT),
+        cost_estimate=pl.CostEstimate(flops=2 << 30, bytes_accessed=4 << 20, transcendentals=0),
+        name="columns",
+    )(blocks, table)
+
+
+def grid_kernel(rows, first_ref, done_ref, block_ref, col_ref, row_ref, before_ref, out_ref, most_ref, half_ref, uv_ref, turned_ref, re_a, im_a, re_b, im_b, label_ref, place_ref, sem):
+    groups, total, depth = done_ref.shape
     sources = total // rows
     per_slot = 2 * PIX // LANES
     quarters = depth // LANES
     for t in range(sources):
         end = (t + 1) * rows
-        label_ref[t : t + 1, :] = block_ref[0, end - 16 : end, :].astype(jnp.float32)[15:16].astype(jnp.int32)
+        for h, ref in enumerate((first_ref, block_ref)):
+            label = ref[0, end - 16 : end, :].astype(jnp.float32)[15:16].astype(jnp.int32)
+            label_ref[t : t + 1, 2 * h * LANES : 2 * (h + 1) * LANES] = label
     fetch = pltpu.make_async_copy(label_ref, place_ref, sem)
     fetch.start()
 
     for g in range(groups):
-        half_ref[g] = jnp.dot(block_ref[g], col_ref[...], preferred_element_type=jnp.float32).astype(jnp.bfloat16)
+        rest = jnp.dot(block_ref[g], col_ref[...], preferred_element_type=jnp.float32).astype(jnp.bfloat16)
+        half_ref[g] = done_ref[g] + rest
     for q in range(quarters):
         left = jnp.concatenate([half_ref[g, :, q * LANES : (q + 1) * LANES] for g in range(groups)], axis=1)
         uv = jnp.dot(left, row_ref[...], preferred_element_type=jnp.float32)
@@ -359,17 +378,17 @@
             out_ref[k, part] = value
 
 
-def first_grid_kernel(rows, block_ref, col_ref, row_ref, *refs):
-    grid_kernel(rows, block_ref, col_ref, row_ref, None, *refs)
-
-
-def place_on_grid(blocks, rows, tables, per_owner, before=None):
-    groups, total, depth = blocks.shape
+def first_grid_kernel(rows, first_ref, done_ref, block_ref, col_ref, row_ref, *refs):
+    grid_kernel(rows, first_ref, done_ref, block_ref, col_ref, row_ref, None, *refs)
+
+
+def place_on_grid(first, done, block, rows, tables, per_owner, before=None):
+    groups, total, depth = done.shape
     sources = total // rows
     shape = (per_owner, 2, TILE_SIDE, TILE_SIDE)
     whole = pl.BlockSpec(memory_space=pltpu.VMEM)
     accumulator = pltpu.VMEM((per_owner * TILE_SIDE, TILE_SIDE), jnp.float32)
-    given = (blocks,) + tables + (() if before is None else (before,))
+    given = (first, done, block) + tables + (() if before is None else (before,))
     return pl.pallas_call(
         functools.partial(first_grid_kernel if before is None else grid_kernel, rows),
         in_specs=[whole] * len(given),
@@ -437,36 +456,48 @@
     per_owner = NT // owners
     full = per_owner * groups * (2 * count // NT)
     rows = -(-full * 3 // 64) * 16
-    local = PIX // groups
-    halves = local // LANES
-
-    part = lax.dynamic_slice_in_dim(screens, corr * local, local, axis=2)
-    part = part.reshape(-1, fields, halves, LANES).transpose(0, 2, 1, 3).reshape(-1, fields * local)
-    all_screens = lax.all_gather(part, "tile", axis=0, tiled=True)
+    halves = PIX // (groups * LANES)
+
+    screen_parts = []
+    for h in range(halves):
+        part = lax.dynamic_slice_in_dim(screens, (corr * halves + h) * LANES, LANES, axis=2)
+        screen_parts.append(lax.all_gather(part.reshape(-1, fields * LANES), "tile", axis=0, tiled=True))
 
     images = make_images(visibilities, coords, stations, tile_ids, offsets, groups)
-    images = lax.all_to_all(images, "corr", split_axis=0, concat_axis=0, tiled=True)
-    images = images.reshape(groups * count, -1)
+    images = [lax.all_to_all(part, "corr", split_axis=0, concat_axis=0, tiled=True) for part in images]
+    images = [part.reshape(groups * count, -1) for part in images]
+    facts = images[0]
 
     taper = jnp.asarray(taper_table(1.0 / nvis)).reshape(groups, halves, 1, LANES)
     taper = lax.dynamic_index_in_dim(taper, corr, axis=0, keepdims=False)
-    tables = tuple(jnp.asarray(table) for table in uv_tables(groups))
+    col_table, row_table = uv_tables(groups)
+    col_tables = [jnp.asarray(col_table[h * 2 * LANES : (h + 1) * 2 * LANES]) for h in range(halves)]
+    row_table = jnp.asarray(row_table)
 
     def exchange(sending, rows):
         received = lax.all_to_all(
-            sending.reshape(groups * owners, rows, 2 * local), ("corr", "tile"), split_axis=0, concat_axis=0, tiled=True
+            sending.reshape(groups * owners, rows, -1), ("corr", "tile"), split_axis=0, concat_axis=0, tiled=True
         )
-        return received.reshape(groups, owners * rows, 2 * local)
-
-    sending, blocks = apply_aterms(images, all_screens, taper, ncorr, owners, per_owner, (0, rows))
-    grid, most = place_on_grid(exchange(sending, rows), rows, tables, per_owner)
+        return received.reshape(groups, owners * rows, -1)
+
+    def finish(received, rows, before=None):
+        done = transform_columns(received[0], col_tables[0])
+        return place_on_grid(received[0], done, received[1], rows, (col_tables[1], row_table), per_owner, before)
+
+    received = []
+    blocks = []
+    for h in range(halves):
+        sending, block = apply_aterms(facts, images[h], screen_parts[h], taper[h], ncorr, owners, per_owner, (0, rows), h)
+        received.append(exchange(sending, rows))
+        blocks.append(block)
+    grid, most = finish(received, rows)
     slots = rows - 1
     if slots < full:
         more = -(-(full - slots + 1) // 16) * 16
 
         def overflow(grid):
-            rest = send_rest(images, blocks, ncorr, owners, per_owner, (slots, more))
-            return place_on_grid(exchange(rest, more), more, tables, per_owner, grid)[0]
+            rest = [send_rest(facts, blocks[h], ncorr, owners, per_owner, (slots, more), h) for h in range(halves)]
+            return finish([exchange(part, more) for part in rest], more, grid)[0]
 
         grid = lax.cond(most[0] > slots, overflow, lambda grid: grid, grid)
     return grid[None]

time: 113 us -> 121 us (1.071)
  blocking collectives: 43.6 us -> 0 us
  waiting for transfers between devices: 13.7 us -> 48.1 us
  starting transfers between devices: 5.16 us -> 16.2 us
  Pallas kernels: 27.1 us -> 30.3 us
  local copies, waits for them, and re-layouts: 7.93 us -> 10.5 us
    all_to_all x1 -> x0, blocking collectives: 43.6 us -> none  [exchange(): lax.all_to_all(sending.reshape(groups * owners, rows, 2 * local), ('corr'...]
    all_to_all x1 -> x4, waiting for transfers between devices: 13.7 us -> 44.2 us  [the longest x2 34.1 us: exchange(): lax.all_to_all(sending.reshape(groups * owners, rows, -1), ('corr', 'tile...]
    all_to_all x1 -> x4, starting transfers between devices: 5.16 us -> 16.2 us  [the longest x2 8.63 us: per_device(): lax.all_to_all(part, 'corr', split_axis=0, concat_axis=0, tiled=True)]
    all_gather x1 -> x2, waiting for transfers between devices: 0.01 us -> 3.82 us  [per_device(): lax.all_gather(part.reshape(-1, fields * LANES), 'tile', axis=0, tiled=True)]
    unnamed x18 -> x29, local copies, waits for them, and re-layouts: 7.21 us -> 8.87 us
    pallas_call x0 -> x1, Pallas kernels: none -> 1.57 us  [transform_columns(): pl.pallas_call(column_kernel, out_shape=jax.ShapeDtypeStruct((groups, tot...]
    pallas_call x1 -> x2, Pallas kernels: 5.04 us -> 6.34 us  [apply_aterms(): pl.pallas_call(functools.partial(aterm_kernel, ncorr, owners, per_owner,...]
  transfers between devices with their start and end apart: 2 -> 6, of which waited for: 1 -> 5; matrix products, arithmetic and copies ran while one was open for 4% -> 1% of each run, Pallas kernels for 11% -> 17%
where the time goes in v2:
time: 121 us; the launch traced here: 119 us
  waiting for transfers between devices  48.1 us (40%)
  Pallas kernels  30.3 us (25%)
  starting transfers between devices  16.2 us (13%)
  between operations  14.3 us (12%)
  local copies, waits for them, and re-layouts  10.5 us (9%)
    all_to_all x2, waiting for transfers between devices, exchange(): lax.all_to_all(sending.reshape(groups * owners, rows, -1), ('corr', 'tile...  34.1 us
    pallas_call x1, Pallas kernels, make_images(): pl.pallas_call(functools.partial(image_kernel, ncorr, groups), grid=(coun...  11.8 us
    pallas_call x1, Pallas kernels, place_on_grid(): pl.pallas_call(functools.partial(first_grid_kernel if before is None else...  10.5 us
    all_to_all x2, waiting for transfers between devices, per_device(): lax.all_to_all(part, 'corr', split_axis=0, concat_axis=0, tiled=True)  10.1 us
    unnamed x29, local copies, waits for them, and re-layouts  8.87 us
    all_to_all x2, starting transfers between devices, per_device(): lax.all_to_all(part, 'corr', split_axis=0, concat_axis=0, tiled=True)  8.63 us
    all_to_all x2, starting transfers between devices, exchange(): lax.all_to_all(sending.reshape(groups * owners, rows, -1), ('corr', 'tile...  7.54 us
    pallas_call x2, Pallas kernels, apply_aterms(): pl.pallas_call(functools.partial(aterm_kernel, ncorr, owners, per_owner,...  6.34 us
  transfers between devices with their start and end apart: 6, of which 5 were waited for; matrix products, arithmetic and copies ran while one was open for 1% of the time, Pallas kernels for 17%

profile of v2, /device:TPU:0, one launch (start us, length us, event | category | flops | bytes accessed | tf_op | source)
XLA Modules:
  0.0 119.3 jit_solution(9194112078018788832)
XLA Ops:
  6.5 1.0 constant_dynamic-slice_fusion.1
  7.5 0.7 copy.18
  8.3 0.9 copy-done.2
  9.2 0.9 copy-done.3
  10.1 0.7 copy-done.4
  10.8 0.7 copy-done.5
  12.1 11.8 %images.1 = (bf16[4,64,1152]{2,1,0:T(8,128)(2,1)}, bf16[4,64,1024]{2,1,0:T(8,128)(2,1)}) custom-call(bf16[64,8,256]{2,1,0:T(8,128)(2,1)S(1)} %copy-done.2, f32[3,64,256]{2,1,0:T(8,128)S(1)} %bitcast.36, s32[2,64]{1,0:T(2,128)S(1)} %bitcast.37, s32[1,64]{1,0:T(1,128)S(1)} %bitcast.39, s32[2,64]{1,0:T(2,128)S(1)} %bitcast.38), custom_call_target="tpu_custom_call" | custom-call | flops 8589934592 | bytes 2097152 | tf_op jit(solution)/shard_map/images/pallas_call | solution.py:127
  24.0 5.2 %all-to-all-start.2 = ((bf16[4,64,1152]{2,1,0:T(8,128)(2,1)}), bf16[4,64,1152]{2,1,0:T(8,128)(2,1)S(1)}, u32[]{:S(2)}, u32[]{:S(2)}) async-start(bf16[4,64,1152]{2,1,0:T(8,128)(2,1)} %get-tuple-element.41), calls=%async_computation.2 | async-start | bytes 1179648 | tf_op jit(solution)/shard_map/all_to_all | solution.py:467
  29.9 8.0 %all-to-all-done.2 = bf16[4,64,1152]{2,1,0:T(8,128)(2,1)S(1)} async-done(((bf16[4,64,1152]{2,1,0:T(8,128)(2,1)}), bf16[4,64,1152]{2,1,0:T(8,128)(2,1)S(1)}, u32[]{:S(2)}, u32[]{:S(2)}) %all-to-all-start.2) | async-done | bytes 589856 | tf_op jit(solution)/shard_map/all_to_all | solution.py:467
  37.9 3.5 %all-to-all-start.4 = ((bf16[4,64,1024]{2,1,0:T(8,128)(2,1)}), bf16[4,64,1024]{2,1,0:T(8,128)(2,1)S(1)}, u32[]{:S(2)}, u32[]{:S(2)}) async-start(bf16[4,64,1024]{2,1,0:T(8,128)(2,1)} %get-tuple-element.43), calls=%async_computation.4 | async-start | bytes 1048576 | tf_op jit(solution)/shard_map/all_to_all | solution.py:467
  41.3 0.7 fusion
  42.0 1.3 %copy-done = bf16[512,1024]{1,0:T(8,128)(2,1)S(1)} copy-done((bf16[512,1024]{1,0:T(8,128)(2,1)S(1)}, bf16[512,1024]{1,0:T(8,128)(2,1)}, u32[]{:S(2)}) %copy-start) | copy-done | bytes 1048600
  43.3 3.2 %aterms.2 = (bf16[4,384,256]{2,1,0:T(8,128)(2,1)}, bf16[256,1024]{1,0:T(8,128)(2,1)}) custom-call(bf16[256,1152]{1,0:T(8,128)(2,1)S(1)} %bitcast.40, f32[1,128]{1,0:T(1,128)S(1)} %get-tuple-element.53.taper_ref, bf16[256,1152]{1,0:T(8,128)(2,1)S(1)} %bitcast.41, bf16[512,1024]{1,0:T(8,128)(2,1)S(1)} %copy-done), custom_call_target="tpu_custom_call" | custom-call | flops 3221225472 | bytes 4194304 | tf_op jit(solution)/shard_map/aterms/pallas_call | solution.py:247
  46.5 2.1 %all-to-all-done.4 = bf16[4,64,1024]{2,1,0:T(8,128)(2,1)S(1)} async-done(((bf16[4,64,1024]{2,1,0:T(8,128)(2,1)}), bf16[4,64,1024]{2,1,0:T(8,128)(2,1)S(1)}, u32[]{:S(2)}, u32[]{:S(2)}) %all-to-all-start.4) | async-done | bytes 524320 | tf_op jit(solution)/shard_map/all_to_all | solution.py:467
  48.5 4.9 %all-to-all-start.3 = ((bf16[32,48,256]{2,1,0:T(8,128)(2,1)}), bf16[32,48,256]{2,1,0:T(8,128)(2,1)S(1)}, u32[]{:S(2)}, u32[]{:S(2)}) async-start(bf16[32,48,256]{2,1,0:T(8,128)(2,1)} %bitcast.12), calls=%async_computation.3 | async-start | bytes 1572864 | tf_op jit(solution)/shard_map/all_to_all | solution.py:478
  53.5 3.8 %all-gather.5.cloned.1.call-done.screen_ref = bf16[512,1024]{1,0:T(8,128)(2,1)} async-done(((bf16[64,1024]{1,0:T(8,128)(2,1)}), bf16[512,1024]{1,0:T(8,128)(2,1)}) %all-gather.5.cloned.1.call-update) | async-done | bytes 1048592 | tf_op jit(solution)/shard_map/all_gather | solution.py:464
  57.3 1.2 %copy-done.1 = bf16[512,1024]{1,0:T(8,128)(2,1)S(1)} copy-done((bf16[512,1024]{1,0:T(8,128)(2,1)S(1)}, bf16[512,1024]{1,0:T(8,128)(2,1)}, u32[]{:S(2)}) %copy-start.1) | copy-done | bytes 1048600
  58.5 3.2 %aterms.3 = (bf16[4,384,256]{2,1,0:T(8,128)(2,1)}, bf16[256,1024]{1,0:T(8,128)(2,1)}) custom-call(bf16[256,1152]{1,0:T(8,128)(2,1)S(1)} %bitcast.42, f32[1,128]{1,0:T(1,128)S(1)} %get-tuple-element.52.taper_ref, bf16[256,1024]{1,0:T(8,128)(2,1)S(1)} %bitcast.35, bf16[512,1024]{1,0:T(8,128)(2,1)S(1)} %copy-done.1), custom_call_target="tpu_custom_call" | custom-call | flops 3221225472 | bytes 4194304 | tf_op jit(solution)/shard_map/aterms/pallas_call | solution.py:247
  61.7 13.8 %all-to-all-done.3 = bf16[32,48,256]{2,1,0:T(8,128)(2,1)S(1)} async-done(((bf16[32,48,256]{2,1,0:T(8,128)(2,1)}), bf16[32,48,256]{2,1,0:T(8,128)(2,1)S(1)}, u32[]{:S(2)}, u32[]{:S(2)}) %all-to-all-start.3) | async-done | bytes 786464 | tf_op jit(solution)/shard_map/all_to_all | solution.py:478
  75.4 2.6 %all-to-all-start.5 = ((bf16[32,48,256]{2,1,0:T(8,128)(2,1)}), bf16[32,48,256]{2,1,0:T(8,128)(2,1)S(1)}, u32[]{:S(2)}, u32[]{:S(2)}) async-start(bf16[32,48,256]{2,1,0:T(8,128)(2,1)} %bitcast.16), calls=%async_computation.5 | async-start | bytes 1572864 | tf_op jit(solution)/shard_map/all_to_all | solution.py:478
  78.1 1.6 %columns.3.done_ref = bf16[4,384,512]{2,1,0:T(8,128)(2,1)S(1)} custom-call(bf16[4,384,256]{2,1,0:T(8,128)(2,1)S(1)} %bitcast.29, bf16[256,512]{1,0:T(8,128)(2,1)} %constant.34.clone.col_ref), custom_call_target="tpu_custom_call" | custom-call | flops 2147483648 | bytes 4194304 | tf_op jit(solution)/shard_map/columns/pallas_call | solution.py:296
  79.6 20.4 %all-to-all-done.5 = bf16[32,48,256]{2,1,0:T(8,128)(2,1)S(1)} async-done(((bf16[32,48,256]{2,1,0:T(8,128)(2,1)}), bf16[32,48,256]{2,1,0:T(8,128)(2,1)S(1)}, u32[]{:S(2)}, u32[]{:S(2)}) %all-to-all-start.5) | async-done | bytes 786464 | tf_op jit(solution)/shard_map/all_to_all | solution.py:478
  100.0 10.5 %grid.3 = (f32[8,2,128,128]{3,2,1,0:T(8,128)S(1)}, s32[1]{0:T(128)}) custom-call(bf16[4,384,256]{2,1,0:T(8,128)(2,1)S(1)} %bitcast.30, bf16[4,384,512]{2,1,0:T(8,128)(2,1)S(1)} %columns.3.done_ref, bf16[4,384,256]{2,1,0:T(8,128)(2,1)S(1)} %bitcast.31, bf16[256,512]{1,0:T(8,128)(2,1)S(1)} %copy-done.11, bf16[512,512]{1,0:T(8,128)(2,1)} %constant.36.clone.row_ref), custom_call_target="tpu_custom_call" | custom-call | tf_op jit(solution)/shard_map/grid/pallas_call | solution.py:392
  111.4 1.0 copy.23
  (27 shorter events, 1.6 us)
Async XLA Ops:
  6.5 35.5 %all-gather.3.cloned.1.call-start = ((), (), s32[]{:S(2)}) async-start(), calls=%async_computation.6 | async-start | bytes 1179648 | tf_op jit(solution)/shard_map/all_gather | solution.py:464
  8.2 1.0 copy-start.2
  9.2 0.9 copy-start.3
  10.1 0.7 copy-start.4
  10.8 0.7 copy-start.5
  11.5 0.7 copy-start.6
  24.0 13.9 %all-to-all-start.2 = ((bf16[4,64,1152]{2,1,0:T(8,128)(2,1)}), bf16[4,64,1152]{2,1,0:T(8,128)(2,1)S(1)}, u32[]{:S(2)}, u32[]{:S(2)}) async-start(bf16[4,64,1152]{2,1,0:T(8,128)(2,1)} %get-tuple-element.41), calls=%async_computation.2 | async-start | bytes 1179648 | tf_op jit(solution)/shard_map/all_to_all | solution.py:467
  29.1 28.1 %all-gather.5.cloned.1.call-start = ((), (), s32[]{:S(2)}) async-start(), calls=%async_computation.7 | async-start | bytes 1179648 | tf_op jit(solution)/shard_map/all_gather | solution.py:464
  37.9 19.4 %copy-start.7 = (bf16[4,64,1152]{2,1,0:T(8,128)(2,1)}, bf16[4,64,1152]{2,1,0:T(8,128)(2,1)S(1)}, u32[]{:S(2)}) copy-start(bf16[4,64,1152]{2,1,0:T(8,128)(2,1)S(1)} %all-to-all-done.2) | copy-start | bytes 1769476
  37.9 10.7 %all-to-all-start.4 = ((bf16[4,64,1024]{2,1,0:T(8,128)(2,1)}), bf16[4,64,1024]{2,1,0:T(8,128)(2,1)S(1)}, u32[]{:S(2)}, u32[]{:S(2)}) async-start(bf16[4,64,1024]{2,1,0:T(8,128)(2,1)} %get-tuple-element.43), calls=%async_computation.4 | async-start | bytes 1048576 | tf_op jit(solution)/shard_map/all_to_all | solution.py:467
  42.0 1.3 %copy-start = (bf16[512,1024]{1,0:T(8,128)(2,1)S(1)}, bf16[512,1024]{1,0:T(8,128)(2,1)}, u32[]{:S(2)}) copy-start(bf16[512,1024]{1,0:T(8,128)(2,1)} %all-gather.3.cloned.1.call-done.screen_ref) | copy-start | bytes 3145732
  48.5 26.9 %all-to-all-start.3 = ((bf16[32,48,256]{2,1,0:T(8,128)(2,1)}), bf16[32,48,256]{2,1,0:T(8,128)(2,1)S(1)}, u32[]{:S(2)}, u32[]{:S(2)}) async-start(bf16[32,48,256]{2,1,0:T(8,128)(2,1)} %bitcast.12), calls=%async_computation.3 | async-start | bytes 1572864 | tf_op jit(solution)/shard_map/all_to_all | solution.py:478
  57.3 1.2 %copy-start.1 = (bf16[512,1024]{1,0:T(8,128)(2,1)S(1)}, bf16[512,1024]{1,0:T(8,128)(2,1)}, u32[]{:S(2)}) copy-start(bf16[512,1024]{1,0:T(8,128)(2,1)} %all-gather.5.cloned.1.call-done.screen_ref) | copy-start | bytes 3145732
  75.4 24.6 %all-to-all-start.5 = ((bf16[32,48,256]{2,1,0:T(8,128)(2,1)}), bf16[32,48,256]{2,1,0:T(8,128)(2,1)S(1)}, u32[]{:S(2)}, u32[]{:S(2)}) async-start(bf16[32,48,256]{2,1,0:T(8,128)(2,1)} %bitcast.16), calls=%async_computation.5 | async-start | bytes 1572864 | tf_op jit(solution)/shard_map/all_to_all | solution.py:478
  78.1 22.0 %copy-start.11 = (bf16[256,512]{1,0:T(8,128)(2,1)S(1)}, bf16[256,512]{1,0:T(8,128)(2,1)}, u32[]{:S(2)}) copy-start(bf16[256,512]{1,0:T(8,128)(2,1)} %constant.35.clone.col_ref) | copy-start | bytes 786436
  110.6 1.8 %copy-start.10 = (f32[8,2,128,128]{3,2,1,0:T(8,128)}, f32[8,2,128,128]{3,2,1,0:T(8,128)S(1)}, u32[]{:S(2)}) copy-start(f32[8,2,128,128]{3,2,1,0:T(8,128)S(1)} %get-tuple-element.46) | copy-start | bytes 3145732
  110.6 1.8 %copy-start.8 = (bf16[4,64,1152]{2,1,0:T(8,128)(2,1)S(1)}, bf16[4,64,1152]{2,1,0:T(8,128)(2,1)}, u32[]{:S(2)}) copy-start(bf16[4,64,1152]{2,1,0:T(8,128)(2,1)} %copy-done.7) | copy-start | bytes 1769476
  110.6 1.8 %copy-start.12 = (bf16[256,1024]{1,0:T(8,128)(2,1)S(1)}, bf16[256,1024]{1,0:T(8,128)(2,1)}, u32[]{:S(2)}) copy-start(bf16[256,1024]{1,0:T(8,128)(2,1)} %get-tuple-element.57) | copy-start | bytes 1572868
  110.6 1.9 %copy-start.13 = (bf16[256,1024]{1,0:T(8,128)(2,1)S(1)}, bf16[256,1024]{1,0:T(8,128)(2,1)}, u32[]{:S(2)}) copy-start(bf16[256,1024]{1,0:T(8,128)(2,1)} %get-tuple-element.59) | copy-start | bytes 1572868
Sparse Core Ops, SparseCore 0:
  9.0 24.8 all-gather.2
  35.5 21.7 all-gather.4

commit v3 on v1

--- a/solution.py
+++ b/solution.py
@@ -14,7 +14,8 @@
 TILE_SIDE = 128
 PIX = SUB * SUB
 LANES = 128
-VMEM_LIMIT = 48 * 1024 * 1024
+VMEM_LIMIT = 36 * 1024 * 1024
+VMEM_ALL = 63 * 1024 * 1024 + 512 * 1024
 
 ROOT2 = math.sqrt(2.0)
 
@@ -45,7 +46,9 @@
     return 1.0 - s * s, s * c
 
 
-def image_kernel(ncorr, groups, vis_ref, coord_ref, station_ref, tile_ref, offset_ref, out_ref, square):
+def image_kernel(ncorr, groups, begin, vis_ref, coord_ref, station_ref, tile_ref, offset_ref, *refs):
+    out_refs, square = refs[:-1], refs[-1]
+    me = lax.axis_index("corr")
     step = vis_ref.shape[0]
     nvis = vis_ref.shape[2]
     centred = (lax.broadcasted_iota(jnp.int32, (SUB, nvis), 0) - SUB // 2).astype(jnp.float32) * (1.0 / SUB)
@@ -53,9 +56,9 @@
     rows = ncorr * SUB
 
     def one(s):
-        u = coord_ref[s, 0:1, :]
-        v = coord_ref[s, 1:2, :]
-        w = coord_ref[s, 2:3, :]
+        u = coord_ref[0, pl.ds(s, 1), :]
+        v = coord_ref[1, pl.ds(s, 1), :]
+        w = coord_ref[2, pl.ds(s, 1), :]
         sag = w * bend
         e_re, e_im = cis_turns(u * centred - sag)
         f_re, f_im = cis_turns(v * centred - sag)
@@ -86,55 +89,62 @@
     lane = lax.broadcasted_iota(jnp.int32, (step, LANES), 1)
     per_tile = LANES // SUB
     halves = SUB // groups // per_tile
-    for g in range(groups):
+    for d in range(groups):
+        first = (me ^ d) * (halves * per_tile)
         for h in range(halves):
             for e in range(ncorr):
                 real = None
                 imag = None
                 for j in range(per_tile):
-                    r = (g * halves + h) * per_tile + j
-                    piece = square[pl.ds(e * SUB + r, step, stride=rows), :]
+                    piece = square[pl.ds(first + (e * SUB + h * per_tile + j), step, stride=rows), :]
                     a = piece if j == 0 else pltpu.roll(piece, SUB * j, 1)
                     b = piece if j == 1 else pltpu.roll(piece, (SUB * (j - 1)) % LANES, 1)
                     keep = lane < SUB * (j + 1)
                     real = a if real is None else jnp.where(lane < SUB * j, real, a)
                     imag = b if imag is None else jnp.where(lane < SUB * j, imag, b)
                 base = h * 2 * ncorr * LANES
-                out_ref[g, :, base + e * LANES : base + (e + 1) * LANES] = real.astype(jnp.bfloat16)
-                out_ref[g, :, base + (ncorr + e) * LANES : base + (ncorr + e + 1) * LANES] = imag.astype(jnp.bfloat16)
-    near = station_ref[:, 0:1]
-    far = station_ref[:, 1:2]
-    facts = (tile_ref[...], offset_ref[:, 0:1], offset_ref[:, 1:2], near // 256, near % 256, far // 256, far % 256)
-    table = jnp.zeros((step, LANES), jnp.int32)
+                out_refs[d][:, base + e * LANES : base + (e + 1) * LANES] = real.astype(jnp.bfloat16)
+                out_refs[d][:, base + (ncorr + e) * LANES : base + (ncorr + e + 1) * LANES] = imag.astype(jnp.bfloat16)
+    near = station_ref[0:1]
+    far = station_ref[1:2]
+    facts = (tile_ref[...], offset_ref[0:1], offset_ref[1:2], near // 256, near % 256, far // 256, far % 256)
+    count = near.shape[1]
+    field = lax.broadcasted_iota(jnp.int32, (LANES, count), 0)
+    table = jnp.zeros((LANES, count), jnp.int32)
     for i, fact in enumerate(facts):
-        table = jnp.where(lane == i, fact, table)
+        table = jnp.where(field == i, fact, table)
+    mine = lax.broadcasted_iota(jnp.int32, (step, count), 0) + (pl.program_id(0) + begin) * step
+    mine = (mine == lax.broadcasted_iota(jnp.int32, (step, count), 1)).astype(jnp.float32).astype(jnp.bfloat16)
     table = table.astype(jnp.float32).astype(jnp.bfloat16)
-    for g in range(groups):
-        out_ref[g, :, 2 * ncorr * halves * LANES :] = table
-
-
-def make_images(visibilities, coords, stations, tile_ids, offsets, groups):
+    table = lax.dot_general(mine, table, (((1,), (1,)), ((), ())), preferred_element_type=jnp.float32)
+    for out_ref in out_refs:
+        out_ref[:, 2 * ncorr * halves * LANES :] = table.astype(jnp.bfloat16)
+
+
+def make_images(visibilities, coords, stations, tile_ids, offsets, groups, part, parts):
     count, fields, nvis = visibilities.shape
     ncorr = fields // 2
     step = 16
     width = fields * PIX // groups + LANES
+    size = count // parts
+    begin = part * size // step
     return pl.pallas_call(
-        functools.partial(image_kernel, ncorr, groups),
-        grid=(count // step,),
+        functools.partial(image_kernel, ncorr, groups, begin),
+        grid=(size // step,),
         in_specs=[
-            pl.BlockSpec((step, fields, nvis), lambda i: (i, 0, 0)),
-            pl.BlockSpec((step, 3, nvis), lambda i: (i, 0, 0)),
-            pl.BlockSpec((step, 2), lambda i: (i, 0)),
-            pl.BlockSpec((step, 1), lambda i: (i, 0)),
-            pl.BlockSpec((step, 2), lambda i: (i, 0)),
+            pl.BlockSpec((step, fields, nvis), lambda i: (i + begin, 0, 0)),
+            pl.BlockSpec((3, step, nvis), lambda i: (0, i + begin, 0)),
+            pl.BlockSpec((2, count), lambda i: (0, 0)),
+            pl.BlockSpec((1, count), lambda i: (0, 0)),
+            pl.BlockSpec((2, count), lambda i: (0, 0)),
         ],
-        out_specs=pl.BlockSpec((groups, step, width), lambda i: (0, i, 0)),
-        out_shape=jax.ShapeDtypeStruct((groups, count, width), jnp.bfloat16),
+        out_specs=[pl.BlockSpec((step, width), lambda i: (i, 0))] * groups,
+        out_shape=[jax.ShapeDtypeStruct((size, width), jnp.bfloat16)] * groups,
         scratch_shapes=[pltpu.VMEM((step * ncorr * SUB, LANES), jnp.float32)],
-        compiler_params=pltpu.CompilerParams(vmem_limit_bytes=VMEM_LIMIT),
-        cost_estimate=pl.CostEstimate(flops=count * 2 * 128 * 512 * 256, bytes_accessed=2 << 20, transcendentals=0),
+        compiler_params=pltpu.CompilerParams(vmem_limit_bytes=VMEM_ALL),
+        cost_estimate=pl.CostEstimate(flops=size << 27, bytes_accessed=2 << 20, transcendentals=0),
         name="images",
-    )(visibilities, coords, stations, tile_ids, offsets)
+    )(visibilities, jnp.transpose(coords, (1, 0, 2)), stations.T, tile_ids.T, offsets.T)
 
 
 def send_rows(owners, per_owner, window, half, facts, block_ref, out_ref):
@@ -183,25 +193,43 @@
             out_ref[e, end - 16 : end, :] = jnp.where(last, labels[o], moved[end - 16 : end]).astype(jnp.bfloat16)
 
 
-def aterm_kernel(ncorr, owners, per_owner, window, facts_ref, taper_ref, image_ref, screen_ref, out_ref, block_ref, near_ref, far_ref):
-    n = image_ref.shape[0]
-    nst = screen_ref.shape[0]
-    facts = facts_ref[...].astype(jnp.float32)
+def aterm_kernel(ncorr, owners, per_owner, window, groups, *refs):
+    pieces = (len(refs) - 8) // 2
+    facts_refs, refs = refs[:pieces], refs[pieces:]
+    image_refs, refs = refs[:pieces], refs[pieces:]
+    taper_ref, mine_ref, other_ref, out_ref, block_ref, facts_ref, near_ref, far_ref = refs
+    count = image_refs[0].shape[0]
+    n = pieces * count
+    share_of = n // groups
+    nst = mine_ref.shape[0] + other_ref.shape[0]
+    me = lax.axis_index("corr")
+    for p in range(pieces):
+        at = pl.multiple_of((me ^ (p % groups)) * share_of + p // groups * count, count)
+        facts_ref[pl.ds(at, count), :] = facts_refs[p][...].astype(jnp.float32)
+    facts = facts_ref[...]
     number = lax.broadcasted_iota(jnp.int32, (n, nst), 1).astype(jnp.float32)
+    share = float(nst // owners)
+    side = (lax.axis_index("tile") & 1).astype(jnp.float32)
     for column, ref in ((3, near_ref), (5, far_ref)):
         station = facts[:, column : column + 1] * 256.0 + facts[:, column + 1 : column + 2]
+        holder = jnp.floor(station * (1.0 / share))
+        pair = jnp.floor(holder * 0.5)
+        station = station - (holder - pair) * share + jnp.where(holder - 2.0 * pair == side, 0.0, float(nst // 2))
         pick = (number == station).astype(jnp.float32).astype(jnp.bfloat16)
-        ref[...] = jnp.dot(pick, screen_ref[...], preferred_element_type=jnp.float32)
+        screens = jnp.concatenate([mine_ref[...], other_ref[...]], axis=0)
+        ref[...] = jnp.dot(pick, screens, preferred_element_type=jnp.float32)
     taper = taper_ref[0]
     chunk = 16
 
     def part(ref, rows, field):
         return ref[rows, field * LANES : (field + 1) * LANES].astype(jnp.float32)
 
-    def body(i, carry):
-        rows = pl.ds(pl.multiple_of(i * chunk, chunk), chunk)
-        image_re = [part(image_ref, rows, e) for e in range(ncorr)]
-        image_im = [part(image_ref, rows, ncorr + e) for e in range(ncorr)]
+    def body(p, i, carry):
+        held = pl.ds(pl.multiple_of(i * chunk, chunk), chunk)
+        at = (me ^ (p % groups)) * share_of + p // groups * count + i * chunk
+        rows = pl.ds(pl.multiple_of(at, chunk), chunk)
+        image_re = [part(image_refs[p], held, e) for e in range(ncorr)]
+        image_im = [part(image_refs[p], held, ncorr + e) for e in range(ncorr)]
         for row_out in range(2):
             mid_re = []
             mid_im = []
@@ -230,45 +258,50 @@
                 block_ref[rows, place + LANES : place + 2 * LANES] = (t_im * taper).astype(jnp.bfloat16)
         return carry
 
-    lax.fori_loop(0, n // chunk, body, 0)
+    for p in range(pieces):
+        lax.fori_loop(0, count // chunk, functools.partial(body, p), 0)
     send_rows(owners, per_owner, window, pl.program_id(0), facts, block_ref, out_ref)
 
 
-def apply_aterms(images, screens, taper, ncorr, owners, per_owner, window):
-    n = images.shape[0]
-    nst = screens.shape[0]
+def apply_aterms(images, groups, mine, other, taper, ncorr, owners, per_owner, window):
+    count = images[0].shape[0]
+    n = count * len(images)
     half = 2 * ncorr * LANES
-    halves = screens.shape[1] // half
+    halves = mine.shape[1] // half
     rows = owners * window[1]
     return pl.pallas_call(
-        functools.partial(aterm_kernel, ncorr, owners, per_owner, window),
+        functools.partial(aterm_kernel, ncorr, owners, per_owner, window, groups),
         grid=(halves,),
-        in_specs=[
-            pl.BlockSpec((n, LANES), lambda h: (0, halves * 2 * ncorr)),
+        in_specs=[pl.BlockSpec((count, LANES), lambda h: (0, halves * 2 * ncorr))] * len(images)
+        + [pl.BlockSpec((count, half), lambda h: (0, h))] * len(images)
+        + [
             pl.BlockSpec((1, 1, LANES), lambda h: (h, 0, 0)),
-            pl.BlockSpec((n, half), lambda h: (0, h)),
-            pl.BlockSpec((nst, half), lambda h: (0, h)),
+            pl.BlockSpec((mine.shape[0], half), lambda h: (0, h)),
+            pl.BlockSpec((other.shape[0], half), lambda h: (0, h)),
         ],
         out_specs=[
             pl.BlockSpec((ncorr, rows, 2 * LANES), lambda h: (0, 0, h)),
             pl.BlockSpec((n, half), lambda h: (0, h)),
+            pl.BlockSpec((n, LANES), lambda h: (0, 0)),
         ],
         out_shape=[
             jax.ShapeDtypeStruct((ncorr, rows, halves * 2 * LANES), jnp.bfloat16),
             jax.ShapeDtypeStruct((n, halves * half), jnp.bfloat16),
+            jax.ShapeDtypeStruct((n, LANES), jnp.float32),
         ],
         scratch_shapes=[pltpu.VMEM((n, half), jnp.float32), pltpu.VMEM((n, half), jnp.float32)],
         compiler_params=pltpu.CompilerParams(vmem_limit_bytes=VMEM_LIMIT),
+        cost_estimate=pl.CostEstimate(flops=6 << 30, bytes_accessed=8 << 20, transcendentals=0),
         name="aterms",
-    )(images, taper, images, screens)
+    )(*images, *images, taper, mine, other)
 
 
 def rest_kernel(owners, per_owner, window, facts_ref, block_ref, out_ref):
-    send_rows(owners, per_owner, window, pl.program_id(0), facts_ref[...].astype(jnp.float32), block_ref, out_ref)
-
-
-def send_rest(images, blocks, ncorr, owners, per_owner, window):
-    n = images.shape[0]
+    send_rows(owners, per_owner, window, pl.program_id(0), facts_ref[...], block_ref, out_ref)
+
+
+def send_rest(facts, blocks, ncorr, owners, per_owner, window):
+    n = blocks.shape[0]
     half = 2 * ncorr * LANES
     halves = blocks.shape[1] // half
     rows = owners * window[1]
@@ -276,14 +309,14 @@
         functools.partial(rest_kernel, owners, per_owner, window),
         grid=(halves,),
         in_specs=[
-            pl.BlockSpec((n, LANES), lambda h: (0, halves * 2 * ncorr)),
+            pl.BlockSpec((n, LANES), lambda h: (0, 0)),
             pl.BlockSpec((n, half), lambda h: (0, h)),
         ],
         out_specs=pl.BlockSpec((ncorr, rows, 2 * LANES), lambda h: (0, 0, h)),
         out_shape=jax.ShapeDtypeStruct((ncorr, rows, halves * 2 * LANES), jnp.bfloat16),
         compiler_params=pltpu.CompilerParams(vmem_limit_bytes=VMEM_LIMIT),
         name="rest",
-    )(images, blocks)
+    )(facts, blocks)
 
 
 def grid_kernel(rows, block_ref, col_ref, row_ref, before_ref, out_ref, most_ref, half_ref, uv_ref, turned_ref, re_a, im_a, re_b, im_b, label_ref, place_ref, sem):
@@ -442,11 +475,16 @@
 
     part = lax.dynamic_slice_in_dim(screens, corr * local, local, axis=2)
     part = part.reshape(-1, fields, halves, LANES).transpose(0, 2, 1, 3).reshape(-1, fields * local)
-    all_screens = lax.all_gather(part, "tile", axis=0, tiled=True)
-
-    images = make_images(visibilities, coords, stations, tile_ids, offsets, groups)
-    images = lax.all_to_all(images, "corr", split_axis=0, concat_axis=0, tiled=True)
-    images = images.reshape(groups * count, -1)
+    sides = [[i for i in range(owners) if i % 2 == side] for side in range(2)]
+    mine = lax.all_gather(part, "tile", axis=0, tiled=True, axis_index_groups=sides)
+
+    images = []
+    for half in range(2):
+        made = make_images(visibilities, coords, stations, tile_ids, offsets, groups, half, 2)
+        for d, piece in enumerate(made):
+            images.append(lax.ppermute(piece, "corr", [(i, i ^ d) for i in range(groups)]) if d else piece)
+    mine, *images = lax.optimization_barrier((mine, *images))
+    other = lax.ppermute(mine, "tile", [(i, i ^ 1) for i in range(owners)])
 
     taper = jnp.asarray(taper_table(1.0 / nvis)).reshape(groups, halves, 1, LANES)
     taper = lax.dynamic_index_in_dim(taper, corr, axis=0, keepdims=False)
@@ -458,14 +496,14 @@
         )
         return received.reshape(groups, owners * rows, 2 * local)
 
-    sending, blocks = apply_aterms(images, all_screens, taper, ncorr, owners, per_owner, (0, rows))
+    sending, blocks, facts = apply_aterms(images, groups, mine, other, taper, ncorr, owners, per_owner, (0, rows))
     grid, most = place_on_grid(exchange(sending, rows), rows, tables, per_owner)
     slots = rows - 1
     if slots < full:
         more = -(-(full - slots + 1) // 16) * 16
 
         def overflow(grid):
-            rest = send_rest(images, blocks, ncorr, owners, per_owner, (slots, more))
+            rest = send_rest(facts, blocks, ncorr, owners, per_owner, (slots, more))
             return place_on_grid(exchange(rest, more), more, tables, per_owner, grid)[0]
 
         grid = lax.cond(most[0] > slots, overflow, lambda grid: grid, grid)

time: 113 us -> 112 us (level)
  starting transfers between devices: 5.16 us -> 8 us
  Pallas kernels: 27.1 us -> 29.5 us
  waiting for transfers between devices: 13.7 us -> 11.3 us
  local copies, waits for them, and re-layouts: 7.93 us -> 5.8 us
    all_to_all x1 -> x0, waiting for transfers between devices: 13.7 us -> none  [per_device(): lax.all_to_all(images, 'corr', split_axis=0, concat_axis=0, tiled=True)]
    ppermute x0 -> x7, waiting for transfers between devices: none -> 8.8 us  [the longest x6 6.62 us: per_device(): lax.ppermute(piece, 'corr', [(i, i ^ d) for i in range(groups)])]
    ppermute x0 -> x7, starting transfers between devices: none -> 8 us  [the longest x6 8 us: per_device(): lax.ppermute(piece, 'corr', [(i, i ^ d) for i in range(groups)])]
    all_to_all x1 -> x0, starting transfers between devices: 5.16 us -> none  [per_device(): lax.all_to_all(images, 'corr', split_axis=0, concat_axis=0, tiled=True)]
    unnamed x18 -> x14, local copies, waits for them, and re-layouts: 7.21 us -> 4.15 us
    all_gather x1, waiting for transfers between devices: 0.01 us -> 2.52 us  [per_device(): lax.all_gather(part, 'tile', axis=0, tiled=True, axis_index_groups=sides)]
    pallas_call x1 -> x2, Pallas kernels: 12.2 us -> 14.1 us  [make_images(): pl.pallas_call(functools.partial(image_kernel, ncorr, groups, begin), gri...]
  transfers between devices with their start and end apart: 2 -> 8, of which waited for: 1 -> 4; matrix products, arithmetic and copies ran while one was open for 4% -> 1% of each run, Pallas kernels for 11% -> 13%
where the time goes in v3:
time: 112 us; the launch traced here: 111 us
  blocking collectives  42.7 us (38%)
  Pallas kernels  29.5 us (26%)
  between operations  14.1 us (13%)
  waiting for transfers between devices  11.3 us (10%)
  starting transfers between devices  8 us (7%)
  local copies, waits for them, and re-layouts  5.8 us (5%)
    all_to_all x1, blocking collectives, exchange(): lax.all_to_all(sending.reshape(groups * owners, rows, 2 * local), ('corr'...  42.7 us
    pallas_call x2, Pallas kernels, make_images(): pl.pallas_call(functools.partial(image_kernel, ncorr, groups, begin), gri...  14.1 us
    pallas_call x1, Pallas kernels, place_on_grid(): pl.pallas_call(functools.partial(first_grid_kernel if before is None else...  9.61 us
    ppermute x6, starting transfers between devices, per_device(): lax.ppermute(piece, 'corr', [(i, i ^ d) for i in range(groups)])  8 us
    ppermute x6, waiting for transfers between devices, per_device(): lax.ppermute(piece, 'corr', [(i, i ^ d) for i in range(groups)])  6.62 us
    pallas_call x1, Pallas kernels, apply_aterms(): pl.pallas_call(functools.partial(aterm_kernel, ncorr, owners, per_owner,...  5.77 us
    unnamed x14, local copies, waits for them, and re-layouts  4.15 us
    all_gather x1, waiting for transfers between devices, per_device(): lax.all_gather(part, 'tile', axis=0, tiled=True, axis_index_groups=sides)  2.52 us
  transfers between devices with their start and end apart: 8, of which 4 were waited for; matrix products, arithmetic and copies ran while one was open for 1% of the time, Pallas kernels for 13%

profile of v3, /device:TPU:0, one launch (start us, length us, event | category | flops | bytes accessed | tf_op | source)
XLA Modules:
  0.0 111.5 jit_solution(11221708342122406399)
XLA Ops:
  6.5 1.0 constant_dynamic-slice_fusion.1
  7.5 0.8 copy.14
  8.3 0.0 all-gather.2.cloned.1.call-update
  8.3 7.1 %images.3 = (bf16[32,2176]{1,0:T(8,128)(2,1)}, bf16[32,2176]{1,0:T(8,128)(2,1)}, bf16[32,2176]{1,0:T(8,128)(2,1)}, bf16[32,2176]{1,0:T(8,128)(2,1)}) custom-call(bf16[64,8,256]{2,1,0:T(8,128)(2,1)} %vis_ref.3, f32[3,64,256]{2,1,0:T(8,128)} %bitcast.28, s32[2,64]{1,0:T(2,128)} %bitcast.30, s32[1,64]{1,0:T(1,128)} %bitcast.34, s32[2,64]{1,0:T(2,128)} %bitcast.32), custom_call_target="tpu_custom_call" | custom-call | flops 4294967296 | bytes 2097152 | tf_op jit(solution)/shard_map/images/pallas_call | solution.py:131
  15.4 3.0 %collective-permute-start.3 = (bf16[32,2176]{1,0:T(8,128)(2,1)}, bf16[32,2176]{1,0:T(8,128)(2,1)S(1)}, u32[]{:S(2)}, u32[]{:S(2)}) collective-permute-start(bf16[32,2176]{1,0:T(8,128)(2,1)} %get-tuple-element.54), channel_id=1, source_target_pairs={{0,8},{8,0},{16,24},{24,16},{1,9},{9,1},{17,25},{25,17},{2,10},{10... | collective-permute-start | bytes 417800 | tf_op jit(solution)/shard_map/ppermute | solution.py:485
  18.3 1.5 %collective-permute-start.4 = (bf16[32,2176]{1,0:T(8,128)(2,1)}, bf16[32,2176]{1,0:T(8,128)(2,1)S(1)}, u32[]{:S(2)}, u32[]{:S(2)}) collective-permute-start(bf16[32,2176]{1,0:T(8,128)(2,1)} %get-tuple-element.55), channel_id=1, source_target_pairs={{0,16},{8,24},{16,0},{24,8},{1,17},{9,25},{17,1},{25,9},{2,18},{10... | collective-permute-start | bytes 417800 | tf_op jit(solution)/shard_map/ppermute | solution.py:485
  19.9 0.0 collective-permute-start.5
  19.9 7.1 %images.2 = (bf16[32,2176]{1,0:T(8,128)(2,1)}, bf16[32,2176]{1,0:T(8,128)(2,1)}, bf16[32,2176]{1,0:T(8,128)(2,1)}, bf16[32,2176]{1,0:T(8,128)(2,1)}) custom-call(bf16[64,8,256]{2,1,0:T(8,128)(2,1)} %vis_ref.3, f32[3,64,256]{2,1,0:T(8,128)} %bitcast.29, s32[2,64]{1,0:T(2,128)} %bitcast.31, s32[1,64]{1,0:T(1,128)} %bitcast.35, s32[2,64]{1,0:T(2,128)} %bitcast.33), custom_call_target="tpu_custom_call" | custom-call | flops 4294967296 | bytes 2097152 | tf_op jit(solution)/shard_map/images/pallas_call | solution.py:131
  27.0 1.9 %collective-permute-start = (bf16[32,2176]{1,0:T(8,128)(2,1)}, bf16[32,2176]{1,0:T(8,128)(2,1)S(1)}, u32[]{:S(2)}, u32[]{:S(2)}) collective-permute-start(bf16[32,2176]{1,0:T(8,128)(2,1)} %get-tuple-element.50), channel_id=1, source_target_pairs={{0,8},{8,0},{16,24},{24,16},{1,9},{9,1},{17,25},{25,17},{2,10},{10... | collective-permute-start | bytes 417800 | tf_op jit(solution)/shard_map/ppermute | solution.py:485
  28.9 1.5 %collective-permute-start.1 = (bf16[32,2176]{1,0:T(8,128)(2,1)}, bf16[32,2176]{1,0:T(8,128)(2,1)S(1)}, u32[]{:S(2)}, u32[]{:S(2)}) collective-permute-start(bf16[32,2176]{1,0:T(8,128)(2,1)} %get-tuple-element.51), channel_id=1, source_target_pairs={{0,16},{8,24},{16,0},{24,8},{1,17},{9,25},{17,1},{25,9},{2,18},{10... | collective-permute-start | bytes 417800 | tf_op jit(solution)/shard_map/ppermute | solution.py:485
  30.4 0.0 collective-permute-start.2
  30.5 2.4 %collective-permute-done.refs_1_.refs_9_ = bf16[32,2176]{1,0:T(8,128)(2,1)S(1)} collective-permute-done((bf16[32,2176]{1,0:T(8,128)(2,1)}, bf16[32,2176]{1,0:T(8,128)(2,1)S(1)}, u32[]{:S(2)}, u32[]{:S(2)}) %collective-permute-start) | collective-permute-done | bytes 139296 | tf_op jit(solution)/shard_map/ppermute | solution.py:485
  32.9 4.2 %collective-permute-done.1.refs_2_.refs_10_ = bf16[32,2176]{1,0:T(8,128)(2,1)S(1)} collective-permute-done((bf16[32,2176]{1,0:T(8,128)(2,1)}, bf16[32,2176]{1,0:T(8,128)(2,1)S(1)}, u32[]{:S(2)}, u32[]{:S(2)}) %collective-permute-start.1) | collective-permute-done | bytes 139296 | tf_op jit(solution)/shard_map/ppermute | solution.py:485
  37.1 2.5 %all-gather.2.cloned.1.call-done.refs_17_ = bf16[256,2048]{1,0:T(8,128)(2,1)} async-done(((bf16[64,2048]{1,0:T(8,128)(2,1)}), bf16[256,2048]{1,0:T(8,128)(2,1)}) %all-gather.2.cloned.1.call-update) | async-done | bytes 1048592 | tf_op jit(solution)/shard_map/all_gather | solution.py:479
  39.6 0.7 constant_dynamic-slice_fusion
  40.3 2.2 %collective-permute-done.6.refs_18_ = bf16[256,2048]{1,0:T(8,128)(2,1)S(1)} collective-permute-done((bf16[256,2048]{1,0:T(8,128)(2,1)}, bf16[256,2048]{1,0:T(8,128)(2,1)S(1)}, u32[]{:S(2)}, u32[]{:S(2)}) %collective-permute-start.6) | collective-permute-done | bytes 1048608 | tf_op jit(solution)/shard_map/ppermute | solution.py:487
  42.5 1.2 %copy-done = bf16[256,2048]{1,0:T(8,128)(2,1)S(1)} copy-done((bf16[256,2048]{1,0:T(8,128)(2,1)S(1)}, bf16[256,2048]{1,0:T(8,128)(2,1)}, u32[]{:S(2)}) %copy-start) | copy-done | bytes 1048600
  43.7 0.9 copy-done.1
  44.6 0.9 copy-done.2
  45.5 5.8 %aterms.1 = (bf16[4,384,512]{2,1,0:T(8,128)(2,1)S(1)}, bf16[256,2048]{1,0:T(8,128)(2,1)S(1)}, f32[256,128]{1,0:T(8,128)S(1)}) custom-call(bf16[32,2176]{1,0:T(8,128)(2,1)S(1)} %copy-done.2, bf16[32,2176]{1,0:T(8,128)(2,1)S(1)} %collective-permute-done.refs_1_.refs_9_, bf16[32,2176]{1,0:T(8,128)(2,1)S(1)} %collective-permute-done.1.refs_2_.refs_10_, ...), custom_call_target="tpu_custom_call" | custom-call | flops 6442450944 | bytes 8388608 | tf_op jit(solution)/shard_map/aterms/pallas_call | solution.py:272
  51.3 42.7 %all_to_all.9 = bf16[32,48,512]{2,1,0:T(8,128)(2,1)S(1)} all-to-all(bf16[32,48,512]{2,1,0:T(8,128)(2,1)S(1)} %bitcast.22), channel_id=1, replica_groups=mesh['corr'=4,'tile'=8] {'corr','tile'}, dimensions={0} | all-to-all | bytes 3145728 | tf_op jit(solution)/shard_map/all_to_all | solution.py:494
  94.1 9.6 %grid.3 = (f32[8,2,128,128]{3,2,1,0:T(8,128)S(1)}, s32[1]{0:T(128)}) custom-call(bf16[4,384,512]{2,1,0:T(8,128)(2,1)S(1)} %bitcast.20, bf16[512,512]{1,0:T(8,128)(2,1)S(1)} %copy-done.4, bf16[512,512]{1,0:T(8,128)(2,1)S(1)} %copy-done.3), custom_call_target="tpu_custom_call" | custom-call | tf_op jit(solution)/shard_map/grid/pallas_call | solution.py:406
  104.3 0.1 copy.19
  104.4 0.3 copy-done.5
  (15 shorter events, 0.0 us)
Async XLA Ops:
  6.5 33.1 %all-gather.2.cloned.1.call-start = ((), (), s32[]{:S(2)}) async-start(), calls=%async_computation.2 | async-start | bytes 1310720 | tf_op jit(solution)/shard_map/all_gather | solution.py:479
  15.4 15.0 %collective-permute-start.3 = (bf16[32,2176]{1,0:T(8,128)(2,1)}, bf16[32,2176]{1,0:T(8,128)(2,1)S(1)}, u32[]{:S(2)}, u32[]{:S(2)}) collective-permute-start(bf16[32,2176]{1,0:T(8,128)(2,1)} %get-tuple-element.54), channel_id=1, source_target_pairs={{0,8},{8,0},{16,24},{24,16},{1,9},{9,1},{17,25},{25,17},{2,10},{10... | collective-permute-start | bytes 417800 | tf_op jit(solution)/shard_map/ppermute | solution.py:485
  18.3 12.1 %collective-permute-start.4 = (bf16[32,2176]{1,0:T(8,128)(2,1)}, bf16[32,2176]{1,0:T(8,128)(2,1)S(1)}, u32[]{:S(2)}, u32[]{:S(2)}) collective-permute-start(bf16[32,2176]{1,0:T(8,128)(2,1)} %get-tuple-element.55), channel_id=1, source_target_pairs={{0,16},{8,24},{16,0},{24,8},{1,17},{9,25},{17,1},{25,9},{2,18},{10... | collective-permute-start | bytes 417800 | tf_op jit(solution)/shard_map/ppermute | solution.py:485
  19.9 10.6 %collective-permute-start.5 = (bf16[32,2176]{1,0:T(8,128)(2,1)}, bf16[32,2176]{1,0:T(8,128)(2,1)S(1)}, u32[]{:S(2)}, u32[]{:S(2)}) collective-permute-start(bf16[32,2176]{1,0:T(8,128)(2,1)} %get-tuple-element.56), channel_id=1, source_target_pairs={{0,24},{8,16},{16,8},{24,0},{1,25},{9,17},{17,9},{25,1},{2,26},{10... | collective-permute-start | bytes 417800 | tf_op jit(solution)/shard_map/ppermute | solution.py:485
  27.0 5.9 %collective-permute-start = (bf16[32,2176]{1,0:T(8,128)(2,1)}, bf16[32,2176]{1,0:T(8,128)(2,1)S(1)}, u32[]{:S(2)}, u32[]{:S(2)}) collective-permute-start(bf16[32,2176]{1,0:T(8,128)(2,1)} %get-tuple-element.50), channel_id=1, source_target_pairs={{0,8},{8,0},{16,24},{24,16},{1,9},{9,1},{17,25},{25,17},{2,10},{10... | collective-permute-start | bytes 417800 | tf_op jit(solution)/shard_map/ppermute | solution.py:485
  28.9 8.2 %collective-permute-start.1 = (bf16[32,2176]{1,0:T(8,128)(2,1)}, bf16[32,2176]{1,0:T(8,128)(2,1)S(1)}, u32[]{:S(2)}, u32[]{:S(2)}) collective-permute-start(bf16[32,2176]{1,0:T(8,128)(2,1)} %get-tuple-element.51), channel_id=1, source_target_pairs={{0,16},{8,24},{16,0},{24,8},{1,17},{9,25},{17,1},{25,9},{2,18},{10... | collective-permute-start | bytes 417800 | tf_op jit(solution)/shard_map/ppermute | solution.py:485
  30.4 6.7 %collective-permute-start.2 = (bf16[32,2176]{1,0:T(8,128)(2,1)}, bf16[32,2176]{1,0:T(8,128)(2,1)S(1)}, u32[]{:S(2)}, u32[]{:S(2)}) collective-permute-start(bf16[32,2176]{1,0:T(8,128)(2,1)} %get-tuple-element.52), channel_id=1, source_target_pairs={{0,24},{8,16},{16,8},{24,0},{1,25},{9,17},{17,9},{25,1},{2,26},{10... | collective-permute-start | bytes 417800 | tf_op jit(solution)/shard_map/ppermute | solution.py:485
  39.6 2.9 %collective-permute-start.6 = (bf16[256,2048]{1,0:T(8,128)(2,1)}, bf16[256,2048]{1,0:T(8,128)(2,1)S(1)}, u32[]{:S(2)}, u32[]{:S(2)}) collective-permute-start(bf16[256,2048]{1,0:T(8,128)(2,1)} %all-gather.2.cloned.1.call-done.refs_17_), channel_id=1, source_target_pairs={{0,1},{1,0},{2,3},{3,2},{4,5},{5,4},{6,7},{7,6},{8,9},{9,8},{10,11... | collective-permute-start | bytes 3145736 | tf_op jit(solution)/shard_map/ppermute | solution.py:487
  42.5 1.2 %copy-start = (bf16[256,2048]{1,0:T(8,128)(2,1)S(1)}, bf16[256,2048]{1,0:T(8,128)(2,1)}, u32[]{:S(2)}) copy-start(bf16[256,2048]{1,0:T(8,128)(2,1)} %all-gather.2.cloned.1.call-done.refs_17_) | copy-start | bytes 3145732
  43.7 0.9 copy-start.1
  44.6 0.9 copy-start.2
  51.3 42.8 %copy-start.3 = (bf16[512,512]{1,0:T(8,128)(2,1)S(1)}, bf16[512,512]{1,0:T(8,128)(2,1)}, u32[]{:S(2)}) copy-start(bf16[512,512]{1,0:T(8,128)(2,1)} %constant.27.clone.row_ref) | copy-start | bytes 1572868
  51.3 42.8 %copy-start.4 = (bf16[512,512]{1,0:T(8,128)(2,1)S(1)}, bf16[512,512]{1,0:T(8,128)(2,1)}, u32[]{:S(2)}) copy-start(bf16[512,512]{1,0:T(8,128)(2,1)} %constant.26.clone.col_ref) | copy-start | bytes 1572868
  103.7 1.0 copy-start.5
Sparse Core Ops, SparseCore 0:
  8.9 30.6 all-gather.1

commit v4 on v3

--- a/solution.py
+++ b/solution.py
@@ -147,10 +147,9 @@
     )(visibilities, jnp.transpose(coords, (1, 0, 2)), stations.T, tile_ids.T, offsets.T)
 
 
-def send_rows(owners, per_owner, window, half, facts, block_ref, out_ref):
+def plan_rows(owners, per_owner, window, facts):
     first, rows = window
     n = facts.shape[0]
-    ncorr = out_ref.shape[0]
     slots = rows - 1
     turned = jnp.transpose(facts)
     owner = jnp.floor(turned[0:1] * (1.0 / per_owner))
@@ -176,48 +175,85 @@
     most = jnp.max(held, axis=0, keepdims=True)
     here = jnp.minimum(jnp.maximum(held - first, 0.0), float(slots))
     lane = lax.broadcasted_iota(jnp.int32, (1, LANES), 1)
-    labels = []
+    labels = ([], [])
     for o in range(owners):
         span = slice(o * LANES, (o + 1) * LANES)
         counts = jnp.where(lane == 0, here[o : o + 1], jnp.where(lane == 1, most, 0.0))
-        left = jnp.where(half == 0, found[0:1, span], found[2:3, span])
-        right = jnp.where(half == 0, found[1:2, span], counts)
-        labels.append(jnp.concatenate([left, right], axis=1))
-    move = chosen(rows)
+        labels[0].append(jnp.concatenate([found[0:1, span], found[1:2, span]], axis=1))
+        labels[1].append(jnp.concatenate([found[2:3, span], counts], axis=1))
+    return chosen(rows), labels
+
+
+def send_rows(owners, rows, move_ref, label_ref, block_ref, out_ref):
     last = lax.broadcasted_iota(jnp.int32, (16, 2 * LANES), 0) == 15
-    for e in range(ncorr):
-        moved = jnp.dot(move, block_ref[:, 2 * e * LANES : 2 * (e + 1) * LANES], preferred_element_type=jnp.float32)
+    for e in range(out_ref.shape[0]):
+        block = block_ref[:, 2 * e * LANES : 2 * (e + 1) * LANES]
+        moved = jnp.dot(move_ref[...], block, preferred_element_type=jnp.float32)
         out_ref[e] = moved.astype(jnp.bfloat16)
         for o in range(owners):
             end = (o + 1) * rows
-            out_ref[e, end - 16 : end, :] = jnp.where(last, labels[o], moved[end - 16 : end]).astype(jnp.bfloat16)
-
-
-def aterm_kernel(ncorr, owners, per_owner, window, groups, *refs):
-    pieces = (len(refs) - 8) // 2
-    facts_refs, refs = refs[:pieces], refs[pieces:]
-    image_refs, refs = refs[:pieces], refs[pieces:]
-    taper_ref, mine_ref, other_ref, out_ref, block_ref, facts_ref, near_ref, far_ref = refs
-    count = image_refs[0].shape[0]
-    n = pieces * count
-    share_of = n // groups
-    nst = mine_ref.shape[0] + other_ref.shape[0]
+            label = label_ref[0, o : o + 1, :]
+            out_ref[e, end - 16 : end, :] = jnp.where(last, label, moved[end - 16 : end]).astype(jnp.bfloat16)
+
+
+def plan_kernel(owners, per_owner, window, groups, *refs):
+    facts_refs, (facts_ref, near_ref, far_ref, move_ref, label_ref) = refs[:-5], refs[-5:]
+    pieces = len(facts_refs)
+    count = facts_refs[0].shape[0]
+    n, nst = near_ref.shape
+    share = n // groups
     me = lax.axis_index("corr")
     for p in range(pieces):
-        at = pl.multiple_of((me ^ (p % groups)) * share_of + p // groups * count, count)
+        at = pl.multiple_of((me ^ (p % groups)) * share + p // groups * count, count)
         facts_ref[pl.ds(at, count), :] = facts_refs[p][...].astype(jnp.float32)
     facts = facts_ref[...]
     number = lax.broadcasted_iota(jnp.int32, (n, nst), 1).astype(jnp.float32)
-    share = float(nst // owners)
-    side = (lax.axis_index("tile") & 1).astype(jnp.float32)
     for column, ref in ((3, near_ref), (5, far_ref)):
         station = facts[:, column : column + 1] * 256.0 + facts[:, column + 1 : column + 2]
-        holder = jnp.floor(station * (1.0 / share))
-        pair = jnp.floor(holder * 0.5)
-        station = station - (holder - pair) * share + jnp.where(holder - 2.0 * pair == side, 0.0, float(nst // 2))
-        pick = (number == station).astype(jnp.float32).astype(jnp.bfloat16)
-        screens = jnp.concatenate([mine_ref[...], other_ref[...]], axis=0)
-        ref[...] = jnp.dot(pick, screens, preferred_element_type=jnp.float32)
+        ref[...] = (number == station).astype(jnp.float32).astype(jnp.bfloat16)
+    move, labels = plan_rows(owners, per_owner, window, facts)
+    move_ref[...] = move
+    for h, rows in enumerate(labels):
+        label_ref[h] = jnp.concatenate(rows, axis=0)
+
+
+def make_plan(images, groups, nst, ncorr, owners, per_owner, window):
+    count, width = images[0].shape
+    n = count * len(images)
+    halves = 2
+    return pl.pallas_call(
+        functools.partial(plan_kernel, owners, per_owner, window, groups),
+        grid=(1,),
+        in_specs=[pl.BlockSpec((count, LANES), lambda i: (0, width // LANES - 1))] * len(images),
+        out_specs=[
+            pl.BlockSpec((n, LANES), lambda i: (0, 0)),
+            pl.BlockSpec((n, nst), lambda i: (0, 0)),
+            pl.BlockSpec((n, nst), lambda i: (0, 0)),
+            pl.BlockSpec((owners * window[1], n), lambda i: (0, 0)),
+            pl.BlockSpec((halves, owners, 2 * LANES), lambda i: (0, 0, 0)),
+        ],
+        out_shape=[
+            jax.ShapeDtypeStruct((n, LANES), jnp.float32),
+            jax.ShapeDtypeStruct((n, nst), jnp.bfloat16),
+            jax.ShapeDtypeStruct((n, nst), jnp.bfloat16),
+            jax.ShapeDtypeStruct((owners * window[1], n), jnp.bfloat16),
+            jax.ShapeDtypeStruct((halves, owners, 2 * LANES), jnp.float32),
+        ],
+        compiler_params=pltpu.CompilerParams(vmem_limit_bytes=VMEM_ALL),
+        cost_estimate=pl.CostEstimate(flops=1 << 30, bytes_accessed=1 << 20, transcendentals=0),
+        name="plan",
+    )(*images)
+
+
+def aterm_kernel(ncorr, owners, rows_of, groups, *refs):
+    pieces = len(refs) - 10
+    image_refs, refs = refs[:pieces], refs[pieces:]
+    taper_ref, screen_ref, near_pick, far_pick, move_ref, label_ref, out_ref, block_ref, near_ref, far_ref = refs
+    count = image_refs[0].shape[0]
+    share_of = pieces * count // groups
+    me = lax.axis_index("corr")
+    for pick, ref in ((near_pick, near_ref), (far_pick, far_ref)):
+        ref[...] = jnp.dot(pick[...], screen_ref[...], preferred_element_type=jnp.float32)
     taper = taper_ref[0]
     chunk = 16
 
@@ -260,44 +296,50 @@
 
     for p in range(pieces):
         lax.fori_loop(0, count // chunk, functools.partial(body, p), 0)
-    send_rows(owners, per_owner, window, pl.program_id(0), facts, block_ref, out_ref)
-
-
-def apply_aterms(images, groups, mine, other, taper, ncorr, owners, per_owner, window):
+    send_rows(owners, rows_of, move_ref, label_ref, block_ref, out_ref)
+
+
+def apply_aterms(images, groups, screens, plan, taper, ncorr, owners, rows):
+    near, far, move, label = plan
     count = images[0].shape[0]
     n = count * len(images)
+    nst = screens.shape[0]
     half = 2 * ncorr * LANES
-    halves = mine.shape[1] // half
-    rows = owners * window[1]
+    halves = screens.shape[1] // half
+    fixed = lambda array: pl.BlockSpec(array.shape, lambda h: (0, 0))
     return pl.pallas_call(
-        functools.partial(aterm_kernel, ncorr, owners, per_owner, window, groups),
+        functools.partial(aterm_kernel, ncorr, owners, rows, groups),
         grid=(halves,),
-        in_specs=[pl.BlockSpec((count, LANES), lambda h: (0, halves * 2 * ncorr))] * len(images)
-        + [pl.BlockSpec((count, half), lambda h: (0, h))] * len(images)
+        in_specs=[pl.BlockSpec((count, half), lambda h: (0, h))] * len(images)
         + [
             pl.BlockSpec((1, 1, LANES), lambda h: (h, 0, 0)),
-            pl.BlockSpec((mine.shape[0], half), lambda h: (0, h)),
-            pl.BlockSpec((other.shape[0], half), lambda h: (0, h)),
+            pl.BlockSpec((nst, half), lambda h: (0, h)),
+            fixed(near),
+            fixed(far),
+            fixed(move),
+            pl.BlockSpec((1, owners, 2 * LANES), lambda h: (h, 0, 0)),
         ],
         out_specs=[
-            pl.BlockSpec((ncorr, rows, 2 * LANES), lambda h: (0, 0, h)),
+            pl.BlockSpec((ncorr, owners * rows, 2 * LANES), lambda h: (0, 0, h)),
             pl.BlockSpec((n, half), lambda h: (0, h)),
-            pl.BlockSpec((n, LANES), lambda h: (0, 0)),
         ],
         out_shape=[
-            jax.ShapeDtypeStruct((ncorr, rows, halves * 2 * LANES), jnp.bfloat16),
+            jax.ShapeDtypeStruct((ncorr, owners * rows, halves * 2 * LANES), jnp.bfloat16),
             jax.ShapeDtypeStruct((n, halves * half), jnp.bfloat16),
-            jax.ShapeDtypeStruct((n, LANES), jnp.float32),
         ],
         scratch_shapes=[pltpu.VMEM((n, half), jnp.float32), pltpu.VMEM((n, half), jnp.float32)],
-        compiler_params=pltpu.CompilerParams(vmem_limit_bytes=VMEM_LIMIT),
+        compiler_params=pltpu.CompilerParams(vmem_limit_bytes=VMEM_ALL),
         cost_estimate=pl.CostEstimate(flops=6 << 30, bytes_accessed=8 << 20, transcendentals=0),
         name="aterms",
-    )(*images, *images, taper, mine, other)
-
-
-def rest_kernel(owners, per_owner, window, facts_ref, block_ref, out_ref):
-    send_rows(owners, per_owner, window, pl.program_id(0), facts_ref[...], block_ref, out_ref)
+    )(*images, taper, screens, near, far, move, label)
+
+
+def rest_kernel(owners, per_owner, window, facts_ref, block_ref, out_ref, move_ref, label_ref):
+    move, labels = plan_rows(owners, per_owner, window, facts_ref[...])
+    move_ref[...] = move
+    for o in range(owners):
+        label_ref[0, o : o + 1, :] = jnp.where(pl.program_id(0) == 0, labels[0][o], labels[1][o])
+    send_rows(owners, window[1], move_ref, label_ref, block_ref, out_ref)
 
 
 def send_rest(facts, blocks, ncorr, owners, per_owner, window):
@@ -308,12 +350,10 @@
     return pl.pallas_call(
         functools.partial(rest_kernel, owners, per_owner, window),
         grid=(halves,),
-        in_specs=[
-            pl.BlockSpec((n, LANES), lambda h: (0, 0)),
-            pl.BlockSpec((n, half), lambda h: (0, h)),
-        ],
+        in_specs=[pl.BlockSpec((n, LANES), lambda h: (0, 0)), pl.BlockSpec((n, half), lambda h: (0, h))],
         out_specs=pl.BlockSpec((ncorr, rows, 2 * LANES), lambda h: (0, 0, h)),
         out_shape=jax.ShapeDtypeStruct((ncorr, rows, halves * 2 * LANES), jnp.bfloat16),
+        scratch_shapes=[pltpu.VMEM((rows, n), jnp.bfloat16), pltpu.VMEM((1, owners, 2 * LANES), jnp.float32)],
         compiler_params=pltpu.CompilerParams(vmem_limit_bytes=VMEM_LIMIT),
         name="rest",
     )(facts, blocks)
@@ -371,8 +411,8 @@
         lax.fori_loop(0, (count + (batch - 1)) // batch, turn, 0)
 
         def add(i, carry):
-            for b in range(4):
-                j = i * 4 + b
+            for b in range(batch):
+                j = i * batch + b
                 row = place_ref[t, 2 * LANES + j] * TILE_SIDE + place_ref[t, j]
                 slot = t * rows + j
                 for part, ref in enumerate((re_a, im_a) if b % 2 == 0 else (re_b, im_b)):
@@ -380,7 +420,7 @@
                     ref[pl.ds(row, SUB), :] = ref[pl.ds(row, SUB), :] + turned_ref[pl.ds(at, SUB), :]
             return carry
 
-        lax.fori_loop(0, (count + 3) // 4, add, 0)
+        lax.fori_loop(0, (count + (batch - 1)) // batch, add, 0)
 
     most_ref[0] = most
     for k in range(out_ref.shape[0]):
@@ -475,17 +515,13 @@
 
     part = lax.dynamic_slice_in_dim(screens, corr * local, local, axis=2)
     part = part.reshape(-1, fields, halves, LANES).transpose(0, 2, 1, 3).reshape(-1, fields * local)
-    sides = [[i for i in range(owners) if i % 2 == side] for side in range(2)]
-    mine = lax.all_gather(part, "tile", axis=0, tiled=True, axis_index_groups=sides)
+    all_screens = lax.all_gather(part, "tile", axis=0, tiled=True)
 
     images = []
     for half in range(2):
         made = make_images(visibilities, coords, stations, tile_ids, offsets, groups, half, 2)
         for d, piece in enumerate(made):
             images.append(lax.ppermute(piece, "corr", [(i, i ^ d) for i in range(groups)]) if d else piece)
-    mine, *images = lax.optimization_barrier((mine, *images))
-    other = lax.ppermute(mine, "tile", [(i, i ^ 1) for i in range(owners)])
-
     taper = jnp.asarray(taper_table(1.0 / nvis)).reshape(groups, halves, 1, LANES)
     taper = lax.dynamic_index_in_dim(taper, corr, axis=0, keepdims=False)
     tables = tuple(jnp.asarray(table) for table in uv_tables(groups))
@@ -496,7 +532,10 @@
         )
         return received.reshape(groups, owners * rows, 2 * local)
 
-    sending, blocks, facts = apply_aterms(images, groups, mine, other, taper, ncorr, owners, per_owner, (0, rows))
+    nst = all_screens.shape[0]
+    facts, *plan = make_plan(images, groups, nst, ncorr, owners, per_owner, (0, rows))
+    all_screens, *plan = lax.optimization_barrier((all_screens, *plan))
+    sending, blocks = apply_aterms(images, groups, all_screens, plan, taper, ncorr, owners, rows)
     grid, most = place_on_grid(exchange(sending, rows), rows, tables, per_owner)
     slots = rows - 1
     if slots < full:

time: 112 us -> 109 us (0.973)
  waiting for transfers between devices: 11.3 us -> 6.25 us
  Pallas kernels: 29.5 us -> 31.8 us
  local copies, waits for them, and re-layouts: 5.8 us -> 4.54 us
    pallas_call x1 -> x2, Pallas kernels: 5.77 us -> 8.29 us  [the longest x1 6.23 us: apply_aterms(): pl.pallas_call(functools.partial(aterm_kernel, ncorr, owners, rows, group...]
    ppermute x1 -> x0, waiting for transfers between devices: 2.19 us -> none  [per_device(): other = lax.ppermute(mine, 'tile', [(i, i ^ 1) for i in range(owners)])]
    unnamed x14 -> x22, local copies, waits for them, and re-layouts: 4.15 us -> 2.31 us
    all_gather x1, waiting for transfers between devices: 2.52 us -> 0.95 us  [per_device(): all_screens = lax.all_gather(part, 'tile', axis=0, tiled=True)]
    ppermute x6, waiting for transfers between devices: 6.62 us -> 5.28 us  [per_device(): lax.ppermute(piece, 'corr', [(i, i ^ d) for i in range(groups)])]
  transfers between devices with their start and end apart: 8 -> 7, of which waited for: 4 -> 3; matrix products, arithmetic and copies ran while one was open for 1% -> 1% of each run, Pallas kernels for 13% -> 15%
where the time goes in v4:
time: 109 us; the launch traced here: 108 us
  blocking collectives  42.9 us (39%)
  Pallas kernels  31.8 us (29%)
  between operations  14.3 us (13%)
  starting transfers between devices  8.04 us (7%)
  waiting for transfers between devices  6.25 us (6%)
  local copies, waits for them, and re-layouts  4.54 us (4%)
    all_to_all x1, blocking collectives, exchange(): lax.all_to_all(sending.reshape(groups * owners, rows, 2 * local), ('corr'...  42.9 us
    pallas_call x2, Pallas kernels, make_images(): pl.pallas_call(functools.partial(image_kernel, ncorr, groups, begin), gri...  14.1 us
    pallas_call x1, Pallas kernels, place_on_grid(): pl.pallas_call(functools.partial(first_grid_kernel if before is None else...  9.42 us
    ppermute x6, starting transfers between devices, per_device(): lax.ppermute(piece, 'corr', [(i, i ^ d) for i in range(groups)])  8.04 us
    pallas_call x1, Pallas kernels, apply_aterms(): pl.pallas_call(functools.partial(aterm_kernel, ncorr, owners, rows, group...  6.23 us
    ppermute x6, waiting for transfers between devices, per_device(): lax.ppermute(piece, 'corr', [(i, i ^ d) for i in range(groups)])  5.28 us
    unnamed x22, local copies, waits for them, and re-layouts  2.31 us
  transfers between devices with their start and end apart: 7, of which 3 were waited for; matrix products, arithmetic and copies ran while one was open for 1% of the time, Pallas kernels for 15%

profile of v4, /device:TPU:0, one launch (start us, length us, event | category | flops | bytes accessed | tf_op | source)
XLA Modules:
  0.0 107.9 jit_solution(5740389393448677019)
XLA Ops:
  6.5 1.0 constant_dynamic-slice_fusion
  7.5 0.8 copy.14
  8.3 0.0 all-gather.2.cloned.1.call-update
  8.3 7.1 %images.3 = (bf16[32,2176]{1,0:T(8,128)(2,1)}, bf16[32,2176]{1,0:T(8,128)(2,1)}, bf16[32,2176]{1,0:T(8,128)(2,1)}, bf16[32,2176]{1,0:T(8,128)(2,1)}) custom-call(bf16[64,8,256]{2,1,0:T(8,128)(2,1)} %vis_ref.3, f32[3,64,256]{2,1,0:T(8,128)} %bitcast.28, s32[2,64]{1,0:T(2,128)} %bitcast.30, s32[1,64]{1,0:T(1,128)} %bitcast.34, s32[2,64]{1,0:T(2,128)} %bitcast.32), custom_call_target="tpu_custom_call" | custom-call | flops 4294967296 | bytes 2097152 | tf_op jit(solution)/shard_map/images/pallas_call | solution.py:131
  15.4 3.0 %collective-permute-start.3 = (bf16[32,2176]{1,0:T(8,128)(2,1)}, bf16[32,2176]{1,0:T(8,128)(2,1)S(1)}, u32[]{:S(2)}, u32[]{:S(2)}) collective-permute-start(bf16[32,2176]{1,0:T(8,128)(2,1)} %get-tuple-element.54), channel_id=1, source_target_pairs={{0,8},{8,0},{16,24},{24,16},{1,9},{9,1},{17,25},{25,17},{2,10},{10... | collective-permute-start | bytes 417800 | tf_op jit(solution)/shard_map/ppermute | solution.py:524
  18.3 1.5 %collective-permute-start.4 = (bf16[32,2176]{1,0:T(8,128)(2,1)}, bf16[32,2176]{1,0:T(8,128)(2,1)S(1)}, u32[]{:S(2)}, u32[]{:S(2)}) collective-permute-start(bf16[32,2176]{1,0:T(8,128)(2,1)} %get-tuple-element.55), channel_id=1, source_target_pairs={{0,16},{8,24},{16,0},{24,8},{1,17},{9,25},{17,1},{25,9},{2,18},{10... | collective-permute-start | bytes 417800 | tf_op jit(solution)/shard_map/ppermute | solution.py:524
  19.9 0.0 collective-permute-start.5
  19.9 7.0 %images.2 = (bf16[32,2176]{1,0:T(8,128)(2,1)}, bf16[32,2176]{1,0:T(8,128)(2,1)}, bf16[32,2176]{1,0:T(8,128)(2,1)}, bf16[32,2176]{1,0:T(8,128)(2,1)}) custom-call(bf16[64,8,256]{2,1,0:T(8,128)(2,1)} %vis_ref.3, f32[3,64,256]{2,1,0:T(8,128)} %bitcast.29, s32[2,64]{1,0:T(2,128)} %bitcast.31, s32[1,64]{1,0:T(1,128)} %bitcast.35, s32[2,64]{1,0:T(2,128)} %bitcast.33), custom_call_target="tpu_custom_call" | custom-call | flops 4294967296 | bytes 2097152 | tf_op jit(solution)/shard_map/images/pallas_call | solution.py:131
  26.9 2.0 %collective-permute-start = (bf16[32,2176]{1,0:T(8,128)(2,1)}, bf16[32,2176]{1,0:T(8,128)(2,1)S(1)}, u32[]{:S(2)}, u32[]{:S(2)}) collective-permute-start(bf16[32,2176]{1,0:T(8,128)(2,1)} %get-tuple-element.50), channel_id=1, source_target_pairs={{0,8},{8,0},{16,24},{24,16},{1,9},{9,1},{17,25},{25,17},{2,10},{10... | collective-permute-start | bytes 417800 | tf_op jit(solution)/shard_map/ppermute | solution.py:524
  28.9 1.5 %collective-permute-start.1 = (bf16[32,2176]{1,0:T(8,128)(2,1)}, bf16[32,2176]{1,0:T(8,128)(2,1)S(1)}, u32[]{:S(2)}, u32[]{:S(2)}) collective-permute-start(bf16[32,2176]{1,0:T(8,128)(2,1)} %get-tuple-element.51), channel_id=1, source_target_pairs={{0,16},{8,24},{16,0},{24,8},{1,17},{9,25},{17,1},{25,9},{2,18},{10... | collective-permute-start | bytes 417800 | tf_op jit(solution)/shard_map/ppermute | solution.py:524
  30.4 0.1 collective-permute-start.2
  30.5 1.3 %constant_dynamic-slice_fusion.1 = f32[1,2,1,128]{3,1,2,0:T(2,128)} fusion(f32[4,2,1,128]{3,1,2,0:T(2,128)} %constant.28, s32[]{:T(128)S(6)} %select_n.7), kind=kLoop, calls=%fused_computation.2 | loop fusion | bytes 2052 | tf_op jit(solution)/shard_map/jit(dynamic_index_in_dim)/dynamic_slice | solution.py:526
  31.8 1.0 collective-permute-done.refs_1_
  32.8 4.2 %collective-permute-done.1.refs_2_ = bf16[32,2176]{1,0:T(8,128)(2,1)S(1)} collective-permute-done((bf16[32,2176]{1,0:T(8,128)(2,1)}, bf16[32,2176]{1,0:T(8,128)(2,1)S(1)}, u32[]{:S(2)}, u32[]{:S(2)}) %collective-permute-start.1) | collective-permute-done | bytes 139296 | tf_op jit(solution)/shard_map/ppermute | solution.py:524
  37.1 0.6 copy-done.8
  37.7 0.1 copy-done.9
  37.8 2.1 %plan.1 = (f32[256,128]{1,0:T(8,128)S(1)}, bf16[256,512]{1,0:T(8,128)(2,1)}, bf16[256,512]{1,0:T(8,128)(2,1)}, bf16[384,256]{1,0:T(8,128)(2,1)}, f32[2,8,256]{2,1,0:T(8,128)}) custom-call(bf16[32,2176]{1,0:T(8,128)(2,1)} %get-tuple-element.49.refs_0_, bf16[32,2176]{1,0:T(8,128)(2,1)} %copy-done.7, bf16[32,2176]{1,0:T(8,128)(2,1)} %copy-done.8, ...), custom_call_target="tpu_custom_call" | custom-call | flops 1073741824 | bytes 1048576 | tf_op jit(solution)/shard_map/plan/pallas_call | solution.py:224
  39.8 0.9 all-gather.2.cloned.1.call-done.refs_9_
  40.8 6.2 %aterms.1 = (bf16[4,384,512]{2,1,0:T(8,128)(2,1)}, bf16[256,2048]{1,0:T(8,128)(2,1)}) custom-call(bf16[32,2176]{1,0:T(8,128)(2,1)} %get-tuple-element.49.refs_0_, bf16[32,2176]{1,0:T(8,128)(2,1)} %copy-done.7, bf16[32,2176]{1,0:T(8,128)(2,1)} %copy-done.8, bf16[32,2176]{1,0:T(8,128)(2,1)} %copy-done.9, bf16[32,2176]{1,0:T(8,128)(2,1)} %get-tuple-element.53.refs_4_, ...), custom_call_target="tpu_custom_call" | custom-call | flops 6442450944 | bytes 8388608 | tf_op jit(solution)/shard_map/aterms/pallas_call | solution.py:310
  47.0 42.9 %all_to_all.9 = bf16[32,48,512]{2,1,0:T(8,128)(2,1)S(1)} all-to-all(bf16[32,48,512]{2,1,0:T(8,128)(2,1)} %bitcast.22), channel_id=1, replica_groups=mesh['corr'=4,'tile'=8] {'corr','tile'}, dimensions={0} | all-to-all | bytes 3145728 | tf_op jit(solution)/shard_map/all_to_all | solution.py:530
  90.0 9.4 %grid.3 = (f32[8,2,128,128]{3,2,1,0:T(8,128)S(1)}, s32[1]{0:T(128)}) custom-call(bf16[4,384,512]{2,1,0:T(8,128)(2,1)S(1)} %bitcast.20, bf16[512,512]{1,0:T(8,128)(2,1)S(1)} %copy-done.1, bf16[512,512]{1,0:T(8,128)(2,1)S(1)} %copy-done), custom_call_target="tpu_custom_call" | custom-call | tf_op jit(solution)/shard_map/grid/pallas_call | solution.py:446
  100.2 0.1 copy.19
  100.3 0.1 copy-done.3
  100.4 0.6 copy-done.2
  (22 shorter events, 0.1 us)
Async XLA Ops:
  6.5 34.3 %all-gather.2.cloned.1.call-start = ((), (), s32[]{:S(2)}) async-start(), calls=%async_computation.2 | async-start | bytes 2359296 | tf_op jit(solution)/shard_map/all_gather | solution.py:518
  15.4 15.0 %collective-permute-start.3 = (bf16[32,2176]{1,0:T(8,128)(2,1)}, bf16[32,2176]{1,0:T(8,128)(2,1)S(1)}, u32[]{:S(2)}, u32[]{:S(2)}) collective-permute-start(bf16[32,2176]{1,0:T(8,128)(2,1)} %get-tuple-element.54), channel_id=1, source_target_pairs={{0,8},{8,0},{16,24},{24,16},{1,9},{9,1},{17,25},{25,17},{2,10},{10... | collective-permute-start | bytes 417800 | tf_op jit(solution)/shard_map/ppermute | solution.py:524
  18.3 13.4 %collective-permute-start.4 = (bf16[32,2176]{1,0:T(8,128)(2,1)}, bf16[32,2176]{1,0:T(8,128)(2,1)S(1)}, u32[]{:S(2)}, u32[]{:S(2)}) collective-permute-start(bf16[32,2176]{1,0:T(8,128)(2,1)} %get-tuple-element.55), channel_id=1, source_target_pairs={{0,16},{8,24},{16,0},{24,8},{1,17},{9,25},{17,1},{25,9},{2,18},{10... | collective-permute-start | bytes 417800 | tf_op jit(solution)/shard_map/ppermute | solution.py:524
  19.9 11.9 %collective-permute-start.5 = (bf16[32,2176]{1,0:T(8,128)(2,1)}, bf16[32,2176]{1,0:T(8,128)(2,1)S(1)}, u32[]{:S(2)}, u32[]{:S(2)}) collective-permute-start(bf16[32,2176]{1,0:T(8,128)(2,1)} %get-tuple-element.56), channel_id=1, source_target_pairs={{0,24},{8,16},{16,8},{24,0},{1,25},{9,17},{17,9},{25,1},{2,26},{10... | collective-permute-start | bytes 417800 | tf_op jit(solution)/shard_map/ppermute | solution.py:524
  26.9 5.9 %collective-permute-start = (bf16[32,2176]{1,0:T(8,128)(2,1)}, bf16[32,2176]{1,0:T(8,128)(2,1)S(1)}, u32[]{:S(2)}, u32[]{:S(2)}) collective-permute-start(bf16[32,2176]{1,0:T(8,128)(2,1)} %get-tuple-element.50), channel_id=1, source_target_pairs={{0,8},{8,0},{16,24},{24,16},{1,9},{9,1},{17,25},{25,17},{2,10},{10... | collective-permute-start | bytes 417800 | tf_op jit(solution)/shard_map/ppermute | solution.py:524
  28.9 8.2 %collective-permute-start.1 = (bf16[32,2176]{1,0:T(8,128)(2,1)}, bf16[32,2176]{1,0:T(8,128)(2,1)S(1)}, u32[]{:S(2)}, u32[]{:S(2)}) collective-permute-start(bf16[32,2176]{1,0:T(8,128)(2,1)} %get-tuple-element.51), channel_id=1, source_target_pairs={{0,16},{8,24},{16,0},{24,8},{1,17},{9,25},{17,1},{25,9},{2,18},{10... | collective-permute-start | bytes 417800 | tf_op jit(solution)/shard_map/ppermute | solution.py:524
  30.4 7.4 %copy-start.4 = (bf16[32,2176]{1,0:T(8,128)(2,1)}, bf16[32,2176]{1,0:T(8,128)(2,1)S(1)}, u32[]{:S(2)}) copy-start(bf16[32,2176]{1,0:T(8,128)(2,1)S(1)} %collective-permute-done.3.refs_5_) | copy-start | bytes 417796
  30.4 6.6 %collective-permute-start.2 = (bf16[32,2176]{1,0:T(8,128)(2,1)}, bf16[32,2176]{1,0:T(8,128)(2,1)S(1)}, u32[]{:S(2)}, u32[]{:S(2)}) collective-permute-start(bf16[32,2176]{1,0:T(8,128)(2,1)} %get-tuple-element.52), channel_id=1, source_target_pairs={{0,24},{8,16},{16,8},{24,0},{1,25},{9,17},{17,9},{25,1},{2,26},{10... | collective-permute-start | bytes 417800 | tf_op jit(solution)/shard_map/ppermute | solution.py:524
  31.8 6.0 %copy-start.5 = (bf16[32,2176]{1,0:T(8,128)(2,1)}, bf16[32,2176]{1,0:T(8,128)(2,1)S(1)}, u32[]{:S(2)}) copy-start(bf16[32,2176]{1,0:T(8,128)(2,1)S(1)} %collective-permute-done.4.refs_6_) | copy-start | bytes 417796
  31.8 5.3 %copy-start.6 = (bf16[32,2176]{1,0:T(8,128)(2,1)}, bf16[32,2176]{1,0:T(8,128)(2,1)S(1)}, u32[]{:S(2)}) copy-start(bf16[32,2176]{1,0:T(8,128)(2,1)S(1)} %collective-permute-done.5.refs_7_) | copy-start | bytes 417796
  32.8 4.3 %copy-start.7 = (bf16[32,2176]{1,0:T(8,128)(2,1)}, bf16[32,2176]{1,0:T(8,128)(2,1)S(1)}, u32[]{:S(2)}) copy-start(bf16[32,2176]{1,0:T(8,128)(2,1)S(1)} %collective-permute-done.refs_1_) | copy-start | bytes 417796
  37.1 0.7 copy-start.8
  37.1 0.7 copy-start.9
  47.0 43.0 %copy-start = (bf16[512,512]{1,0:T(8,128)(2,1)S(1)}, bf16[512,512]{1,0:T(8,128)(2,1)}, u32[]{:S(2)}) copy-start(bf16[512,512]{1,0:T(8,128)(2,1)} %constant.27.clone.row_ref) | copy-start | bytes 1572868
  47.0 43.0 %copy-start.1 = (bf16[512,512]{1,0:T(8,128)(2,1)S(1)}, bf16[512,512]{1,0:T(8,128)(2,1)}, u32[]{:S(2)}) copy-start(bf16[512,512]{1,0:T(8,128)(2,1)} %constant.26.clone.col_ref) | copy-start | bytes 1572868
  99.4 1.0 copy-start.3
  99.4 1.6 %copy-start.2 = (bf16[256,2048]{1,0:T(8,128)(2,1)S(1)}, bf16[256,2048]{1,0:T(8,128)(2,1)}, u32[]{:S(2)}) copy-start(bf16[256,2048]{1,0:T(8,128)(2,1)} %get-tuple-element.75) | copy-start | bytes 3145732
Sparse Core Ops, SparseCore 0:
  9.0 31.7 all-gather.1
